TPU v7x, 512 devices: a whole 4x8x8 slice. The times are simulated.
512 devices in a mesh: ctx: 64 (over z, y_lo, core), tp: 8 (over x, y_hi).
Axes of the slice: x: 4, y: 8 (y_hi: 2, y_lo: 4; y = y_hi * 4 + y_lo), z: 8, core: 2. Of those that a mesh axis runs over, the one named last changes fastest.
Arguments:
- projected: bfloat16 [3, 16384, 8192], P(None, 'ctx', 'tp'), may hold values from -6 to 6
- short_filter: float32 [3, 3, 8192], P(None, None, 'tp'), may hold values from -3.5 to 3.5
- decay_rate: float32 [8192, 16], P('tp'), may hold values from 6.1035156e-06 to 0.033, as said below
- residue: float32 [8192, 16], P('tp')
- skip_gain: float32 [8192], P('tp'), may hold values from -4 to 4
- out_weight: bfloat16 [8192, 4096], P(('tp', 'ctx')), may hold values from -0.25 to 0.25
Outputs:
- block_out: bfloat16 [16384, 4096], P('ctx', 'tp')
Inputs may be any that keep to these rules, and one draw needn't show every extreme that they name: `decay_rate`: positive.
All inputs are finite; a program needn't handle non-finite values.
Results may differ from a plain program's by a relative error of at most 0.017.
Values may be sent and summed in bfloat16 or wider, within the bound.
A program may use at most 128 MiB of HBM per device.

v0:
```python
import math

import jax
import jax.numpy as jnp
from jax import lax
from jax.sharding import PartitionSpec as P

exact_mode = lax.Precision.HIGHEST


def passed_along(value, axis, steps):
    count = lax.axis_size(axis)
    first, last = (max(0, -steps), min(count, count - steps))
    return lax.ppermute(value, axis, [(source, source + steps) for source in range(first, last)])


def dft_table(row_count, col_count, period):
    product = (
        lax.iota(jnp.int32, row_count)[:, None] * lax.iota(jnp.int32, col_count)[None, :] % period
    )
    angle = product.astype(jnp.float32) * (2.0 * math.pi / period)
    return (jnp.cos(angle), -jnp.sin(angle))


def modal_spectrum(rates, weights, length, freq):
    period = 2 * length
    theta = freq * (2.0 * math.pi / period)
    parity = 1.0 - 2.0 * jnp.mod(freq, 2.0)
    half_sin = jnp.sin(0.5 * theta)
    full_sin = jnp.sin(theta)
    total_re = jnp.zeros((), jnp.float32)
    total_im = jnp.zeros((), jnp.float32)
    for pole_index in range(rates.shape[0]):
        rate = rates[pole_index]
        ratio = jnp.exp(-rate)
        numer = 1.0 - jnp.exp(-rate * length) * parity
        denom_re = -jnp.expm1(-rate) + 2.0 * ratio * half_sin * half_sin
        denom_im = ratio * full_sin
        factor = weights[pole_index] * numer / (denom_re * denom_re + denom_im * denom_im)
        total_re = total_re + factor * denom_re
        total_im = total_im - factor * denom_im
    return (total_re, total_im)


def right_mul(left, table):
    return jnp.einsum("ckn,nm->ckm", left, table, precision=exact_mode)


def featurize(projected, short_filter):
    taps = short_filter.shape[1]
    row_count = projected.shape[1]
    rim = projected[:, row_count - (taps - 1) :, :]
    before = passed_along(rim, "ctx", 1)
    padded = jnp.concatenate([before, projected], axis=1).astype(jnp.float32)
    featured = jnp.zeros(projected.shape, jnp.float32)
    for tap_index in range(taps):
        featured = (
            featured
            + short_filter[:, tap_index : tap_index + 1, :]
            * padded[:, taps - 1 - tap_index : taps - 1 - tap_index + row_count, :]
        )
    return featured


def global_filter(by_channel, rate_part, weight_part):
    seq_len, chan_count = by_channel.shape
    total_len = 2 * seq_len
    split_low = max(
        (divisor for divisor in range(1, math.isqrt(total_len) + 1) if total_len % divisor == 0)
    )
    split_high = total_len // split_low
    signal = jnp.concatenate(
        [by_channel.astype(jnp.float32), jnp.zeros((seq_len, chan_count), jnp.float32)], axis=0
    )
    signal = signal.reshape(split_low, split_high, chan_count)
    cos_low, sin_low = dft_table(split_low, split_low, split_low)
    cos_high, sin_high = dft_table(split_high, split_high, split_high)
    twist_cos, twist_sin = dft_table(split_low, split_high, total_len)
    real_a = jnp.einsum("kn,nmc->ckm", cos_low, signal, precision=exact_mode)
    imag_a = jnp.einsum("kn,nmc->ckm", sin_low, signal, precision=exact_mode)
    real_b = real_a * twist_cos - imag_a * twist_sin
    imag_b = real_a * twist_sin + imag_a * twist_cos
    real_c = right_mul(real_b, cos_high) - right_mul(imag_b, sin_high)
    imag_c = right_mul(real_b, sin_high) + right_mul(imag_b, cos_high)
    freq_index = (
        lax.iota(jnp.int32, split_low)[:, None]
        + split_low * lax.iota(jnp.int32, split_high)[None, :]
    )
    spec_re, spec_im = modal_spectrum(
        rate_part.T[:, :, None, None],
        weight_part.T[:, :, None, None],
        seq_len,
        freq_index.astype(jnp.float32),
    )
    real_d = real_c * spec_re - imag_c * spec_im
    imag_d = real_c * spec_im + imag_c * spec_re
    real_e = right_mul(real_d, cos_high) + right_mul(imag_d, sin_high)
    imag_e = right_mul(imag_d, cos_high) - right_mul(real_d, sin_high)
    real_f = real_e * twist_cos + imag_e * twist_sin
    imag_f = imag_e * twist_cos - real_e * twist_sin
    result = jnp.einsum("mk,ckn->cmn", cos_low, real_f, precision=exact_mode) + jnp.einsum(
        "mk,ckn->cmn", sin_low, imag_f, precision=exact_mode
    )
    result = result.reshape(chan_count, total_len)[:, :seq_len] / total_len
    return result.T


def on_device(projected, short_filter, decay_rate, residue, skip_gain, out_weight):
    featured = featurize(projected, short_filter)
    gated = (featured[1] * featured[2]).astype(jnp.bfloat16)
    by_channel = lax.all_to_all(gated, "ctx", split_axis=1, concat_axis=0, tiled=True)
    chan_count = by_channel.shape[1]
    offset = lax.axis_index("ctx") * chan_count
    rate_part = lax.dynamic_slice_in_dim(decay_rate, offset, chan_count, 0)
    weight_part = lax.dynamic_slice_in_dim(residue, offset, chan_count, 0)
    gain_part = lax.dynamic_slice_in_dim(skip_gain, offset, chan_count, 0)
    conv_channel = global_filter(by_channel, rate_part, weight_part) + gain_part[
        None, :
    ] * by_channel.astype(jnp.float32)
    filtered = lax.all_to_all(
        conv_channel.astype(jnp.bfloat16), "ctx", split_axis=0, concat_axis=1, tiled=True
    )
    mixed = (featured[0] * filtered.astype(jnp.float32)).astype(jnp.bfloat16)
    partial_sum = jnp.dot(
        mixed,
        lax.all_gather(out_weight, "ctx", axis=0, tiled=True),
        preferred_element_type=jnp.float32,
    )
    return lax.psum_scatter(partial_sum.astype(jnp.bfloat16), "tp", scatter_dimension=1, tiled=True)


def solution(mesh):
    in_specs = (
        P(None, "ctx", "tp"),
        P(None, None, "tp"),
        P("tp", None),
        P("tp", None),
        P("tp"),
        P(("tp", "ctx"), None),
    )
    out_specs = P("ctx", "tp")
    return jax.shard_map(
        on_device, mesh=mesh, in_specs=in_specs, out_specs=out_specs, check_vma=False
    )
```

profile of v0, /device:TPU:1, one launch (start us, length us, event | category | flops | bytes accessed | tf_op | source)
XLA Modules:
  0.0 282.1 jit_solution(14805983177342153369)
XLA Ops:
  6.5 0.8 slice.162
  7.4 4.6 %collective-permute-start = (bf16[3,2,1024]{2,1,0:T(2,128)(2,1)S(1)}, bf16[3,2,1024]{2,1,0:T(2,128)(2,1)S(1)}, u32[]{:S(2)}, u32[]{:S(2)}) collective-permute-start(bf16[3,2,1024]{2,1,0:T(2,128)(2,1)S(1)} %slice.162), channel_id=1, source_target_pairs={{0,8},{8,16},{16,24},{24,32},{32,40},{40,48},{48,56},{56,64},{64,7... | collective-permute-start | bytes 36872 | tf_op jit(solution)/shard_map/ppermute | solution.py:14
  12.0 0.9 fusion.181
  13.0 1.0 fusion.98
  14.0 0.6 copy_bitcast_fusion.1
  14.6 0.8 dynamic-slice_bitcast_fusion
  15.4 1.7 copy.37
  17.1 0.6 copy.77
  17.7 0.4 copy.36
  18.1 1.0 maximum_convert_fusion
  19.1 3.2 %fusion = f32[3,256,1024]{1,2,0:T(8,128)S(1)} fusion(f32[3,258,1024]{1,2,0:T(8,128)S(1)} %maximum_convert_fusion, f32[3,1024]{1,0:T(4,128)S(1)} %copy-done.3, f32[3,1024]{1,0:T(4,128)S(1)} %copy-done.4, f32[3,1024]{1,0:T(4,128)S(1)} %bitcast.279), kind=kLoop, calls=%fused_computation.2 | loop fusion | flops 3932160 | bytes 12619776 | tf_op jit(solution)/shard_map/add | solution.py:58
  22.3 0.9 fusion.65
  23.2 13.8 %all-to-all-start = ((bf16[256,64,16]{0,2,1:T(8,128)(2,1)}), bf16[256,64,16]{0,2,1:T(8,128)(2,1)}, u32[]{:S(2)}, u32[]{:S(2)}) async-start(bf16[256,64,16]{0,2,1:T(8,128)(2,1)} %bitcast.276), calls=%async_computation | async-start | bytes 1048576 | tf_op jit(solution)/shard_map/all_to_all | solution.py:111
  37.0 0.2 reduce-scatter.2.cloned.1.call-start
  37.2 0.6 exponential_bitcast_fusion.29
  37.8 0.8 copy.43
  38.6 0.1 copy.44
  38.7 0.8 copy.45
  39.4 1.3 dynamic_slice.11
  40.7 0.6 broadcast_multiply_fusion.15
  41.3 0.6 slice_bitcast_fusion.16
  42.0 0.5 sine_negate_fusion.5
  42.5 0.7 exponential_bitcast_fusion.31
  43.2 0.7 negate_bitcast_fusion.15
  43.9 14.0 %all-to-all-done = bf16[256,64,16]{0,2,1:T(8,128)(2,1)} async-done(((bf16[256,64,16]{0,2,1:T(8,128)(2,1)}), bf16[256,64,16]{0,2,1:T(8,128)(2,1)}, u32[]{:S(2)}, u32[]{:S(2)}) %all-to-all-start) | async-done | bytes 524320 | tf_op jit(solution)/shard_map/all_to_all | solution.py:111
  57.9 1.2 convert_bitcast_fusion
  59.1 0.1 concatenate.7
  59.3 0.8 copy-done
  60.1 0.6 copy.69
  60.7 3.6 %fusion.118 = f32[256,16,128]{2,0,1:T(8,128)S(1)} fusion(f32[128,256,16]{1,0,2:T(8,128)S(1)} %bitcast.269), kind=kOutput, calls=%fused_computation.190 | convolution fusion | flops 805552128 | bytes 4194304 | tf_op jit(solution)/shard_map/kn,nmc->ckm/dot_general | solution.py:80
  64.3 3.6 %fusion.121 = f32[256,16,128]{2,0,1:T(8,128)S(1)} fusion(f32[128,256,16]{1,0,2:T(8,128)S(1)} %bitcast.270), kind=kOutput, calls=%fused_computation.193 | convolution fusion | flops 805535744 | bytes 4194304 | tf_op jit(solution)/shard_map/kn,nmc->ckm/dot_general | solution.py:79
  67.9 4.9 %fusion.76 = f32[16,128,256]{2,1,0:T(8,128)S(1)} fusion(f32[256,16,128]{2,0,1:T(8,128)S(1)} %fusion.118, f32[256,16,128]{2,0,1:T(8,128)S(1)} %fusion.121, f32[128,256]{0,1:T(8,128)S(1)} %get-tuple-element.97, f32[128,256]{0,1:T(8,128)S(1)} %get-tuple-element.98), kind=kOutput, calls=%fused_computation.140 | convolution fusion | flops 1613103104 | bytes 6553600 | tf_op jit(solution)/shard_map/ckn,nm->ckm/dot_general | solution.py:46
  72.8 4.6 %fusion.74 = f32[16,128,256]{2,1,0:T(8,128)S(1)} fusion(f32[256,16,128]{2,0,1:T(8,128)S(1)} %fusion.118, f32[256,16,128]{2,0,1:T(8,128)S(1)} %fusion.121, f32[128,256]{0,1:T(8,128)S(1)} %get-tuple-element.97, f32[128,256]{0,1:T(8,128)S(1)} %get-tuple-element.98), kind=kOutput, calls=%fused_computation.139 | convolution fusion | flops 1613168640 | bytes 6553600 | tf_op jit(solution)/shard_map/ckn,nm->ckm/dot_general | solution.py:46
  77.8 4.6 %convolution_subtract_fusion.1 = f32[16,128,256]{2,1,0:T(8,128)S(1)} fusion(f32[16,128,256]{2,1,0:T(8,128)S(1)} %fusion.76, f32[256,16,128]{2,0,1:T(8,128)S(1)} %fusion.118, f32[256,16,128]{2,0,1:T(8,128)S(1)} %fusion.121, f32[128,256]{0,1:T(8,128)S(1)} %get-tuple-element.97, f32[128,256]{0,1:T(8,128)S(1)} %get-tuple-element.98), kind=kOutput, calls=%fused_computation.124 | convolution fusion | flops 1613692928 | bytes 8650752 | tf_op jit(solution)/shard_map/ckn,nm->ckm/dot_general | solution.py:46
  82.9 40.8 %multiply_add_fusion = (f32[16,128,256]{2,1,0:T(8,128)S(1)}, f32[16,128,256]{2,1,0:T(8,128)S(1)}, f32[16,128,256]{2,1,0:T(8,128)S(1)}, f32[16,128,256]{2,1,0:T(8,128)S(1)}) fusion(f32[16,128,256]{2,1,0:T(8,128)S(1)} %convolution_subtract_fusion.1, f32[16]{0:T(128)} %get-tuple-element.29, f32[16]{0:T(128)S(1)} %copy-done.17, f32[16]{0:T(128)} %get-tuple-element.28, ...), kind=kOutput, calls=%fused_computation.102 | convolution fusion | flops 1740505088 | bytes 17437696 | tf_op jit(solution)/shard_map/ckn,nm->ckm/dot_general | solution.py:46
  123.6 3.0 %fusion.85 = f32[16,128,256]{1,2,0:T(8,128)S(1)} fusion(f32[16,128,256]{2,1,0:T(8,128)S(1)} %get-tuple-element.5), kind=kOutput, calls=%fused_computation.152 | convolution fusion | flops 1611530240 | bytes 4194304 | tf_op jit(solution)/shard_map/ckn,nm->ckm/dot_general | solution.py:46
  126.6 0.6 multiply_subtract_fusion
  127.2 3.0 %fusion.87 = f32[16,128,256]{1,2,0:T(8,128)S(1)} fusion(f32[16,128,256]{2,1,0:T(8,128)S(1)} %multiply_subtract_fusion), kind=kOutput, calls=%fused_computation.154 | convolution fusion | flops 1611530240 | bytes 4194304 | tf_op jit(solution)/shard_map/ckn,nm->ckm/dot_general | solution.py:46
  130.2 3.0 %convolution_subtract_fusion = f32[16,128,256]{1,2,0:T(8,128)S(1)} fusion(f32[16,128,256]{1,2,0:T(8,128)S(1)} %fusion.85, f32[16,128,256]{2,1,0:T(8,128)S(1)} %multiply_subtract_fusion), kind=kOutput, calls=%fused_computation.121 | convolution fusion | flops 1612120064 | bytes 6291456 | tf_op jit(solution)/shard_map/ckn,nm->ckm/dot_general | solution.py:46
  133.3 3.4 %convolution_add_fusion = f32[16,128,256]{1,2,0:T(8,128)S(1)} fusion(f32[16,128,256]{1,2,0:T(8,128)S(1)} %fusion.87, f32[16,128,256]{2,1,0:T(8,128)S(1)} %get-tuple-element.5), kind=kOutput, calls=%fused_computation.122 | convolution fusion | flops 1612120064 | bytes 6291456 | tf_op jit(solution)/shard_map/ckn,nm->ckm/dot_general | solution.py:46
  136.6 2.2 fusion.52
  138.9 3.7 %add_bitcast_fusion = f32[16,128,256]{1,2,0:T(8,128)} fusion(f32[16,256,128]{2,1,0:T(8,128)S(1)} %fusion.52, f32[16,128,256]{1,2,0:T(8,128)S(1)} %convolution_subtract_fusion, f32[16,128,256]{1,2,0:T(8,128)S(1)} %convolution_add_fusion, f32[128,256]{0,1:T(8,128)S(1)} %get-tuple-element.97, f32[128,256]{0,1:T(8,128)S(1)} %get-tuple-element.98), kind=kOutput, calls=%fused_computation.93 | convolution fusion | flops 807632896 | bytes 8650752 | tf_op jit(solution)/shard_map/mk,ckn->cmn/dot_general | solution.py:101
  142.6 3.0 %copy.70 = f32[2,8,128,256]{3,1,2,0:T(8,128)} copy(f32[2,8,128,256]{2,3,1,0:T(8,128)} %bitcast.274) | data formatting | bytes 4194304
  145.6 1.7 fusion.64
  147.4 24.8 %all_to_all.23 = bf16[64,256,16]{1,2,0:T(8,128)(2,1)S(1)} all-to-all(bf16[64,256,16]{1,2,0:T(8,128)(2,1)S(1)} %bitcast.277), channel_id=1, replica_groups=mesh['ctx'=64,'tp'=8] {'ctx'}, dimensions={0} | all-to-all | bytes 1048576 | tf_op jit(solution)/shard_map/all_to_all | solution.py:120
  172.2 0.9 fusion.67
  173.2 7.3 %convolution_convert_fusion = bf16[256,4096]{1,0:T(8,128)(2,1)} fusion(bf16[256,1024]{0,1:T(8,128)(2,1)} %fusion.67, bf16[1024,4096]{1,0:T(8,128)(2,1)} %all-gather.2.cloned.1.call-done), kind=kOutput, calls=%fused_computation | convolution fusion | flops 2148532224 | bytes 11010048 | tf_op jit(solution)/shard_map/dot_general | solution.py:124
  180.4 94.6 %reduce-scatter.2.cloned.1.call-done = bf16[256,512]{1,0:T(8,128)(2,1)} async-done(((bf16[256,4096]{1,0:T(8,128)(2,1)}), bf16[256,512]{1,0:T(8,128)(2,1)}) %reduce-scatter.2.cloned.1.call-update) | async-done | bytes 262160 | tf_op jit(solution)/shard_map/reduce_scatter | solution.py:129
  (97 shorter events, 0.3 us)
Async XLA Ops:
  6.5 166.6 %all-gather.2.cloned.1.call-start = ((), (), s32[]{:S(2)}) async-start(), calls=%async_computation.3 | async-start | bytes 8519680 | tf_op jit(solution)/shard_map/all_gather | solution.py:126
  7.4 10.3 %collective-permute-start = (bf16[3,2,1024]{2,1,0:T(2,128)(2,1)S(1)}, bf16[3,2,1024]{2,1,0:T(2,128)(2,1)S(1)}, u32[]{:S(2)}, u32[]{:S(2)}) collective-permute-start(bf16[3,2,1024]{2,1,0:T(2,128)(2,1)S(1)} %slice.162), channel_id=1, source_target_pairs={{0,8},{8,16},{16,24},{24,32},{32,40},{40,48},{48,56},{56,64},{64,7... | collective-permute-start | bytes 36872 | tf_op jit(solution)/shard_map/ppermute | solution.py:14
  18.1 1.0 copy-start.3
  18.1 1.0 copy-start.4
  18.1 1.0 copy-start.5
  23.2 34.6 %all-to-all-start = ((bf16[256,64,16]{0,2,1:T(8,128)(2,1)}), bf16[256,64,16]{0,2,1:T(8,128)(2,1)}, u32[]{:S(2)}, u32[]{:S(2)}) async-start(bf16[256,64,16]{0,2,1:T(8,128)(2,1)} %bitcast.276), calls=%async_computation | async-start | bytes 1048576 | tf_op jit(solution)/shard_map/all_to_all | solution.py:111
  37.0 238.0 %reduce-scatter.2.cloned.1.call-start = ((), (), s32[]{:S(2)}) async-start(), calls=%async_computation.4 | async-start | bytes 2359296 | tf_op jit(solution)/shard_map/reduce_scatter | solution.py:129
  77.4 5.0 %copy-start.1 = (f32[128,256]{1,0:T(8,128)S(1)}, f32[128,256]{1,0:T(8,128)}, u32[]{:S(2)}) copy-start(f32[128,256]{1,0:T(8,128)} %copy.43) | copy-start | bytes 393220
  77.4 5.0 %copy-start.2 = (f32[128,256]{1,0:T(8,128)S(1)}, f32[128,256]{1,0:T(8,128)}, u32[]{:S(2)}) copy-start(f32[128,256]{1,0:T(8,128)} %copy.45) | copy-start | bytes 393220
  77.5 5.0 %copy-start.6 = (f32[16]{0:T(128)S(1)}, f32[16]{0:T(128)}, u32[]{:S(2)}) copy-start(f32[16]{0:T(128)} %get-tuple-element.81) | copy-start | bytes 196
  77.5 5.0 %copy-start.7 = (f32[16]{0:T(128)S(1)}, f32[16]{0:T(128)}, u32[]{:S(2)}) copy-start(f32[16]{0:T(128)} %get-tuple-element.82) | copy-start | bytes 196
  77.5 5.0 %copy-start.8 = (f32[16]{0:T(128)S(1)}, f32[16]{0:T(128)}, u32[]{:S(2)}) copy-start(f32[16]{0:T(128)} %get-tuple-element.83) | copy-start | bytes 196
  77.5 5.0 %copy-start.9 = (f32[16]{0:T(128)S(1)}, f32[16]{0:T(128)}, u32[]{:S(2)}) copy-start(f32[16]{0:T(128)} %get-tuple-element.84) | copy-start | bytes 196
  77.5 5.0 %copy-start.10 = (f32[16]{0:T(128)S(1)}, f32[16]{0:T(128)}, u32[]{:S(2)}) copy-start(f32[16]{0:T(128)} %get-tuple-element.85) | copy-start | bytes 196
  77.5 5.0 %copy-start.11 = (f32[16]{0:T(128)S(1)}, f32[16]{0:T(128)}, u32[]{:S(2)}) copy-start(f32[16]{0:T(128)} %get-tuple-element.86) | copy-start | bytes 196
  77.5 5.0 %copy-start.12 = (f32[16]{0:T(128)S(1)}, f32[16]{0:T(128)}, u32[]{:S(2)}) copy-start(f32[16]{0:T(128)} %get-tuple-element.87) | copy-start | bytes 196
  77.5 5.0 %copy-start.13 = (f32[16]{0:T(128)S(1)}, f32[16]{0:T(128)}, u32[]{:S(2)}) copy-start(f32[16]{0:T(128)} %get-tuple-element.88) | copy-start | bytes 196
  77.5 5.0 %copy-start.14 = (f32[16]{0:T(128)S(1)}, f32[16]{0:T(128)}, u32[]{:S(2)}) copy-start(f32[16]{0:T(128)} %get-tuple-element.89) | copy-start | bytes 196
  77.5 5.0 %copy-start.15 = (f32[16]{0:T(128)S(1)}, f32[16]{0:T(128)}, u32[]{:S(2)}) copy-start(f32[16]{0:T(128)} %get-tuple-element.90) | copy-start | bytes 196
  77.6 5.0 %copy-start.16 = (f32[16]{0:T(128)S(1)}, f32[16]{0:T(128)}, u32[]{:S(2)}) copy-start(f32[16]{0:T(128)} %get-tuple-element.65) | copy-start | bytes 196
  77.6 5.0 %copy-start.17 = (f32[16]{0:T(128)S(1)}, f32[16]{0:T(128)}, u32[]{:S(2)}) copy-start(f32[16]{0:T(128)} %get-tuple-element.66) | copy-start | bytes 196
  77.6 5.0 %copy-start.18 = (f32[16]{0:T(128)S(1)}, f32[16]{0:T(128)}, u32[]{:S(2)}) copy-start(f32[16]{0:T(128)} %get-tuple-element.67) | copy-start | bytes 196
  77.6 5.0 %copy-start.19 = (f32[16]{0:T(128)S(1)}, f32[16]{0:T(128)}, u32[]{:S(2)}) copy-start(f32[16]{0:T(128)} %get-tuple-element.68) | copy-start | bytes 196
  77.6 5.0 %copy-start.20 = (f32[16]{0:T(128)S(1)}, f32[16]{0:T(128)}, u32[]{:S(2)}) copy-start(f32[16]{0:T(128)} %get-tuple-element.69) | copy-start | bytes 196
  77.6 5.0 %copy-start.21 = (f32[16]{0:T(128)S(1)}, f32[16]{0:T(128)}, u32[]{:S(2)}) copy-start(f32[16]{0:T(128)} %get-tuple-element.70) | copy-start | bytes 196
  77.6 5.0 %copy-start.22 = (f32[16]{0:T(128)S(1)}, f32[16]{0:T(128)}, u32[]{:S(2)}) copy-start(f32[16]{0:T(128)} %get-tuple-element.71) | copy-start | bytes 196
  77.6 5.0 %copy-start.23 = (f32[16]{0:T(128)S(1)}, f32[16]{0:T(128)}, u32[]{:S(2)}) copy-start(f32[16]{0:T(128)} %get-tuple-element.72) | copy-start | bytes 196
  77.6 5.0 %copy-start.24 = (f32[16]{0:T(128)S(1)}, f32[16]{0:T(128)}, u32[]{:S(2)}) copy-start(f32[16]{0:T(128)} %get-tuple-element.73) | copy-start | bytes 196
  77.6 5.0 %copy-start.25 = (f32[16]{0:T(128)S(1)}, f32[16]{0:T(128)}, u32[]{:S(2)}) copy-start(f32[16]{0:T(128)} %get-tuple-element.74) | copy-start | bytes 196
  77.7 5.0 %copy-start.26 = (f32[16]{0:T(128)S(1)}, f32[16]{0:T(128)}, u32[]{:S(2)}) copy-start(f32[16]{0:T(128)} %get-tuple-element.75) | copy-start | bytes 196
  77.7 5.0 %copy-start.27 = (f32[16]{0:T(128)S(1)}, f32[16]{0:T(128)}, u32[]{:S(2)}) copy-start(f32[16]{0:T(128)} %get-tuple-element.76) | copy-start | bytes 196
  77.7 5.0 %copy-start.28 = (f32[16]{0:T(128)S(1)}, f32[16]{0:T(128)}, u32[]{:S(2)}) copy-start(f32[16]{0:T(128)} %get-tuple-element.77) | copy-start | bytes 196
  77.7 5.0 %copy-start.29 = (f32[16]{0:T(128)S(1)}, f32[16]{0:T(128)}, u32[]{:S(2)}) copy-start(f32[16]{0:T(128)} %get-tuple-element.78) | copy-start | bytes 196
  77.7 5.0 %copy-start.30 = (f32[16]{0:T(128)S(1)}, f32[16]{0:T(128)}, u32[]{:S(2)}) copy-start(f32[16]{0:T(128)} %get-tuple-element.79) | copy-start | bytes 196
  77.7 5.0 %copy-start.31 = (f32[16]{0:T(128)S(1)}, f32[16]{0:T(128)}, u32[]{:S(2)}) copy-start(f32[16]{0:T(128)} %get-tuple-element.80) | copy-start | bytes 196
  77.7 5.0 %copy-start.32 = (f32[16]{0:T(128)S(1)}, f32[16]{0:T(128)}, u32[]{:S(2)}) copy-start(f32[16]{0:T(128)} %get-tuple-element.11) | copy-start | bytes 196
  77.7 5.0 %copy-start.33 = (f32[16]{0:T(128)S(1)}, f32[16]{0:T(128)}, u32[]{:S(2)}) copy-start(f32[16]{0:T(128)} %get-tuple-element.12) | copy-start | bytes 196
  77.7 5.0 %copy-start.34 = (f32[16]{0:T(128)S(1)}, f32[16]{0:T(128)}, u32[]{:S(2)}) copy-start(f32[16]{0:T(128)} %get-tuple-element.13) | copy-start | bytes 196
  77.7 5.0 %copy-start.35 = (f32[16]{0:T(128)S(1)}, f32[16]{0:T(128)}, u32[]{:S(2)}) copy-start(f32[16]{0:T(128)} %get-tuple-element.14) | copy-start | bytes 196
  77.8 5.0 %copy-start.36 = (f32[16]{0:T(128)S(1)}, f32[16]{0:T(128)}, u32[]{:S(2)}) copy-start(f32[16]{0:T(128)} %get-tuple-element.15) | copy-start | bytes 196
  77.8 5.0 %copy-start.37 = (f32[16]{0:T(128)S(1)}, f32[16]{0:T(128)}, u32[]{:S(2)}) copy-start(f32[16]{0:T(128)} %get-tuple-element.16) | copy-start | bytes 196
  77.8 5.0 %copy-start.38 = (f32[16]{0:T(128)S(1)}, f32[16]{0:T(128)}, u32[]{:S(2)}) copy-start(f32[16]{0:T(128)} %get-tuple-element.17) | copy-start | bytes 196
  77.8 5.0 %copy-start.39 = (f32[16]{0:T(128)S(1)}, f32[16]{0:T(128)}, u32[]{:S(2)}) copy-start(f32[16]{0:T(128)} %get-tuple-element.18) | copy-start | bytes 196
  77.8 5.0 %copy-start.40 = (f32[16]{0:T(128)S(1)}, f32[16]{0:T(128)}, u32[]{:S(2)}) copy-start(f32[16]{0:T(128)} %get-tuple-element.19) | copy-start | bytes 196
  77.8 5.0 %copy-start.41 = (f32[16]{0:T(128)S(1)}, f32[16]{0:T(128)}, u32[]{:S(2)}) copy-start(f32[16]{0:T(128)} %get-tuple-element.20) | copy-start | bytes 196
  77.8 5.0 %copy-start.42 = (f32[16]{0:T(128)S(1)}, f32[16]{0:T(128)}, u32[]{:S(2)}) copy-start(f32[16]{0:T(128)} %get-tuple-element.21) | copy-start | bytes 196
  77.8 5.0 %copy-start.43 = (f32[16]{0:T(128)S(1)}, f32[16]{0:T(128)}, u32[]{:S(2)}) copy-start(f32[16]{0:T(128)} %get-tuple-element.22) | copy-start | bytes 196
  142.6 3.0 %copy-start.44 = (f32[16]{0:T(128)S(1)}, f32[16]{0:T(128)}, u32[]{:S(2)}) copy-start(f32[16]{0:T(128)} %dynamic_slice.11) | copy-start | bytes 196
  (1 other events, 1.0 us)
Sparse Core Ops, SparseCore 0:
  12.1 135.8 all-gather.1
  180.6 94.3 reduce-scatter.1
where the time goes:
time: 287 us; the launch traced here: 282 us
  waiting for transfers between devices  109 us (38%)
  matrix products  87.7 us (31%)
  blocking collectives  24.8 us (9%)
  starting transfers between devices  18.6 us (6%)
  between operations  14.5 us (5%)
  local copies, waits for them, and re-layouts  14.4 us (5%)
  other arithmetic  13.5 us (5%)
    reduce_scatter x1, waiting for transfers between devices, on_device(): lax.psum_scatter(partial_sum.astype(jnp.bfloat16), 'tp', scatter_dimensio...  94.6 us
    dot_general x8, matrix products, right_mul(): return jnp.einsum('ckn,nm->ckm', left, table, precision=exact_mode)  67.3 us
    all_to_all x1, blocking collectives, on_device(): lax.all_to_all(conv_channel.astype(jnp.bfloat16), 'ctx', split_axis=0, co...  24.8 us
    all_to_all x1, waiting for transfers between devices, on_device(): lax.all_to_all(gated, 'ctx', split_axis=1, concat_axis=0, tiled=True)  14 us
    all_to_all x1, starting transfers between devices, on_device(): lax.all_to_all(gated, 'ctx', split_axis=1, concat_axis=0, tiled=True)  13.8 us
    unnamed x95, local copies, waits for them, and re-layouts  7.59 us
    dot_general x1, matrix products, on_device(): jnp.dot(mixed, lax.all_gather(out_weight, 'ctx', axis=0, tiled=True), pre...  7.26 us
  transfers between devices with their start and end apart: 4, of which 2 were waited for; matrix products, arithmetic and copies ran while one was open for 38% of the time, Pallas kernels for 0%

commit v1 on v0

v1 whole, which is shorter than its diff:
```python
import jax
import jax.numpy as jnp
from jax import lax
from jax.experimental import pallas as pl
from jax.experimental.pallas import tpu as pltpu
from jax.sharding import PartitionSpec as P

ZS = 8
PLANE = 8
XS = 4
TOK = 256
CHAN = 1024
LANES = 128
GROUPS = CHAN // LANES
MODES = 16
ROWS = 16
BLOCK = PLANE * ROWS
PIECE = 256
UNROLL = 8


def block_kernel(
    proj,
    filt,
    rate,
    resid,
    skip,
    weight,
    out,
    wq,
    wbuf,
    halo_out,
    halo_in,
    gates,
    query,
    conv,
    decay,
    gain,
    power,
    state,
    stage1,
    total,
    stage2,
    carries,
    carry,
    mixed,
    far_out,
    up_out,
    down_out,
    far_up_in,
    far_down_in,
    up_in,
    down_in,
    half_out,
    half_in,
    halo_sem,
    wy_send,
    wy_recv,
    up_send,
    up_recv,
    dn_send,
    dn_recv,
    s1_send,
    s1_recv,
    s2_send,
    s2_recv,
    s3_send,
    s3_recv,
    mix_send,
    mix_recv,
    x_send,
    x_recv,
    h_send,
    h_recv,
):
    ctx = lax.axis_index("ctx")
    tp = lax.axis_index("tp")
    z = ctx // PLANE
    e = ctx % PLANE
    c = e % 2
    par = (e // 2) % 2
    quad = e // 4
    x = tp // 2
    h = tp % 2

    def at(zz, ee):
        return zz * PLANE + ee

    def member(pp, cc):
        return z * PLANE + quad * 4 + pp * 2 + cc

    def remote(src, dst, send, recv, to_ctx, to_tp):
        return pltpu.make_async_remote_copy(
            src_ref=src,
            dst_ref=dst,
            send_sem=send,
            recv_sem=recv,
            device_id={"ctx": to_ctx, "tp": to_tp},
            device_id_type=pl.DeviceIdType.MESH,
        )

    sent = []

    def start(*args):
        copy = remote(*args)
        copy.start()
        sent.append(copy)

    def arrived(dst, recv):
        remote(dst, dst, recv, recv, at((z + 1) % ZS, e), tp).wait_recv()

    barrier = pltpu.get_barrier_semaphore()

    def greet(to_ctx, to_tp):
        pl.semaphore_signal(
            barrier,
            inc=1,
            device_id={"ctx": to_ctx, "tp": to_tp},
            device_id_type=pl.DeviceIdType.MESH,
        )

    for k in range(1, PLANE):
        greet(at(z, (e + k) % PLANE), tp)
    for k in range(1, ZS):
        greet(at((z + k) % ZS, e), tp)
    for k in (1, XS - 1):
        greet(ctx, ((x + k) % XS) * 2 + h)
    for pp in range(2):
        for cc in range(2):
            greet(member(pp, cc), x * 2 + (1 - h))
    to_next = jnp.logical_and(e == PLANE - 1, z < ZS - 1)
    to_prev = jnp.logical_and(e == 0, z > 0)

    @pl.when(to_next)
    def _():
        greet(ctx + 1, tp)

    @pl.when(to_prev)
    def _():
        greet(ctx - 1, tp)

    for q in range(4):
        pp, cc = q // 2, q % 2
        for xx in range(XS):
            col = xx * 1024 + pp * 512 + cc * PIECE
            wq[q, :, xx * PIECE : (xx + 1) * PIECE] = weight[:, col : col + PIECE]
    rims = [proj[p, TOK - 16 : TOK, :].astype(jnp.float32)[14:16, :] for p in range(3)]
    for p in range(3):
        halo_out[2 * p : 2 * p + 2, :] = rims[p]
    halo_out[6:8, :] = jnp.zeros((2, CHAN), jnp.float32)

    @pl.when(ctx == 0)
    def _():
        halo_in[...] = jnp.zeros_like(halo_in)

    for g in range(GROUPS):
        cols = slice(g * LANES, (g + 1) * LANES)
        decay[pl.ds(g, MODES, stride=GROUPS), :] = jnp.exp(-rate[:, cols])
        power[pl.ds(g, MODES, stride=GROUPS), :] = rate[:, cols]
        gain[pl.ds(g, MODES, stride=GROUPS), :] = resid[:, cols]

    row_id = lax.broadcasted_iota(jnp.int32, (TOK, LANES), 0)

    def featurize(g, carry_in):
        lo = pl.multiple_of(g * LANES, LANES)
        cols = pl.ds(lo, LANES)
        featured = []
        for p in range(3):
            now = proj[p, :, cols].astype(jnp.float32)
            taps = filt[p, :, cols]
            one = jnp.where(row_id >= 1, pltpu.roll(now, 1, 0), 0.0)
            two = jnp.where(row_id >= 2, pltpu.roll(now, 2, 0), 0.0)
            featured.append(taps[0:1, :] * now + taps[1:2, :] * one + taps[2:3, :] * two)
        query[:, cols] = featured[0]
        gates[pl.ds(pl.multiple_of(g * TOK, TOK), TOK), :] = (
            (featured[1] * featured[2]).astype(jnp.bfloat16).astype(jnp.float32)
        )
        return carry_in

    lax.fori_loop(0, GROUPS, featurize, 0)

    beyond = jnp.logical_or(to_next, to_prev).astype(jnp.int32)
    pl.semaphore_wait(barrier, 7 + 7 + 2 + 4 + beyond)

    halo_copy = remote(halo_out, halo_in, halo_sem.at[0], halo_sem.at[1], ctx + 1, tp)

    @pl.when(ctx < ZS * PLANE - 1)
    def _():
        halo_copy.start()

    my_rows = pl.ds(pl.multiple_of(z * BLOCK + e * ROWS, ROWS), ROWS)
    for k in range(1, PLANE):
        ee = (e + k) % PLANE
        share = ((ee // 2) % 2) * 2 + ee % 2
        start(wq.at[share], wbuf.at[my_rows], wy_send.at[k], wy_recv.at[k], at(z, ee), tp)
    wbuf[my_rows, :] = wq[par * 2 + c]

    @pl.when(ctx > 0)
    def _():
        remote(halo_in, halo_in, halo_sem.at[0], halo_sem.at[1], ctx - 1, tp).wait_recv()

    edge_id = lax.broadcasted_iota(jnp.int32, (8, CHAN), 0)
    featured = []
    for p in range(3):
        now = proj[p, 0:16, :].astype(jnp.float32)[0:8, :]
        before2 = halo_in[2 * p : 2 * p + 1, :]
        before1 = halo_in[2 * p + 1 : 2 * p + 2, :]
        one = jnp.where(edge_id >= 1, pltpu.roll(now, 1, 0), before1)
        two = jnp.where(
            edge_id >= 2, pltpu.roll(now, 2, 0), jnp.where(edge_id == 0, before2, before1)
        )
        taps = filt[p]
        featured.append(taps[0:1, :] * now + taps[1:2, :] * one + taps[2:3, :] * two)
    query[0:8, :] = featured[0]
    first = (featured[1] * featured[2]).astype(jnp.bfloat16).astype(jnp.float32)
    for g in range(GROUPS):
        gates[g * TOK : g * TOK + 8, :] = first[:, g * LANES : (g + 1) * LANES]

    def token(ref, t):
        return ref[pl.ds(t, GROUPS, stride=TOK), :]

    def mode(ref, n):
        return ref[n * GROUPS : (n + 1) * GROUPS, :]

    zero = tuple(jnp.zeros((GROUPS, LANES), jnp.float32) for _ in range(MODES))

    def end_state(step, held):
        for u in range(UNROLL):
            g_now = token(gates, step * UNROLL + u)
            held = tuple(mode(decay, n) * held[n] + g_now for n in range(MODES))
        return held

    final = lax.fori_loop(0, TOK // UNROLL, end_state, zero)
    for n in range(MODES):
        state[n * GROUPS : (n + 1) * GROUPS, :] = final[n]

    own_modes = pl.ds(pl.multiple_of(e * 16, 16), 16)
    for k in range(1, PLANE):
        ee = (e + k) % PLANE
        start(
            state.at[pl.ds(pl.multiple_of(ee * 16, 16), 16)],
            stage1.at[e],
            s1_send.at[k],
            s1_recv.at[k],
            at(z, ee),
            tp,
        )
    stage1[e] = state[own_modes, :]

    for k in range(1, PLANE):
        ee = (e + PLANE - k) % PLANE
        arrived(
            wbuf.at[pl.ds(pl.multiple_of(z * BLOCK + ee * ROWS, ROWS), ROWS)], wy_recv.at[k]
        )
    half = BLOCK // 2

    def piece(zz, second):
        return wbuf.at[pl.ds(pl.multiple_of(zz * BLOCK + second * half, half), half)]

    def ring_wait(m):
        s = m // 2
        arrived(piece((z + 2 * ZS - 1 - s) % ZS, m % 2), up_recv.at[m])
        arrived(piece((z + 1 + s) % ZS, 1 - m % 2), dn_recv.at[m])

    def ring_send(m):
        if m >= 2:
            ring_wait(m - 2)
        s = m // 2
        up = piece((z + ZS - s) % ZS, m % 2)
        start(up, up, up_send.at[m], up_recv.at[m], at((z + 1) % ZS, e), tp)
        down = piece((z + s) % ZS, 1 - m % 2)
        start(down, down, dn_send.at[m], dn_recv.at[m], at((z + ZS - 1) % ZS, e), tp)

    ring_send(0)
    ring_send(1)

    def local_filter(step, held):
        for u in range(UNROLL):
            t = step * UNROLL + u
            g_now = token(gates, t)
            held = tuple(mode(decay, n) * held[n] + g_now for n in range(MODES))
            terms = [mode(gain, n) * held[n] for n in range(MODES)]
            terms.append(skip[...] * g_now)
            while len(terms) > 1:
                terms = [
                    terms[i] + terms[i + 1] if i + 1 < len(terms) else terms[i]
                    for i in range(0, len(terms), 2)
                ]
            conv[pl.ds(t, GROUPS, stride=TOK), :] = terms[0]
        return held

    steps = TOK // UNROLL
    held = lax.fori_loop(0, steps // 2, local_filter, zero)

    for k in range(1, PLANE):
        arrived(stage1.at[(e + PLANE - k) % PLANE], s1_recv.at[k])
    rates = power[own_modes, :]
    over_device = jnp.exp(rates * (-float(TOK)))
    over_plane = jnp.exp(rates * (-float(TOK * PLANE)))
    running = stage1[0]
    for k in range(1, PLANE):
        running = over_device * running + stage1[k]
    total[...] = running
    for k in range(1, ZS):
        start(total, stage2.at[z], s2_send.at[k], s2_recv.at[k], at((z + k) % ZS, e), tp)
    stage2[z] = running

    held = lax.fori_loop(steps // 2, steps, local_filter, held)

    for k in range(1, ZS):
        arrived(stage2.at[(z + ZS - k) % ZS], s2_recv.at[k])
    running = jnp.zeros((16, LANES), jnp.float32)
    for k in range(ZS - 1):
        running = jnp.where(k < z, over_plane * running + stage2[k], running)
    for k in range(PLANE):
        carries[k] = running
        if k < PLANE - 1:
            running = over_device * running + stage1[k]
    for k in range(1, PLANE):
        ee = (e + k) % PLANE
        start(carries.at[ee], carry.at[own_modes], s3_send.at[k], s3_recv.at[k], at(z, ee), tp)
    carry[own_modes, :] = carries[e]

    ring_send(2)
    ring_send(3)

    for k in range(1, PLANE):
        ee = (e + PLANE - k) % PLANE
        arrived(carry.at[pl.ds(pl.multiple_of(ee * 16, 16), 16)], s3_recv.at[k])

    def add_carry(step, held):
        for u in range(UNROLL):
            t = step * UNROLL + u
            held = tuple(mode(decay, n) * held[n] for n in range(MODES))
            terms = list(held) + [token(conv, t)]
            while len(terms) > 1:
                terms = [
                    terms[i] + terms[i + 1] if i + 1 < len(terms) else terms[i]
                    for i in range(0, len(terms), 2)
                ]
            conv[pl.ds(t, GROUPS, stride=TOK), :] = terms[0]
        return held

    lax.fori_loop(
        0, steps, add_carry, tuple(mode(gain, n) * mode(carry, n) for n in range(MODES))
    )

    def token_rows(pp, cc):
        return pl.ds(pl.multiple_of((pp * 2 + cc) * TOK, TOK), TOK)

    mine = token_rows(par, c)

    def mix(g, carry_in):
        cols = pl.ds(pl.multiple_of(g * LANES, LANES), LANES)
        filtered = conv[pl.ds(pl.multiple_of(g * TOK, TOK), TOK), :].astype(jnp.bfloat16)
        mixed[mine, cols] = (query[:, cols] * filtered.astype(jnp.float32)).astype(jnp.bfloat16)
        return carry_in

    lax.fori_loop(0, GROUPS, mix, 0)

    start(mixed.at[mine], mixed.at[mine], mix_send.at[0], mix_recv.at[0], member(par, 1 - c), tp)
    start(mixed.at[mine], mixed.at[mine], mix_send.at[1], mix_recv.at[1], member(1 - par, c), tp)

    ring_send(4)
    ring_send(5)
    across = token_rows(1 - par, c)
    arrived(mixed.at[across], mix_recv.at[1])
    start(
        mixed.at[across], mixed.at[across], mix_send.at[2], mix_recv.at[2], member(par, 1 - c), tp
    )
    ring_send(6)
    ring_wait(5)
    ring_wait(6)
    arrived(mixed.at[token_rows(par, 1 - c)], mix_recv.at[0])

    def product(m, d):
        rows = pl.ds(pl.multiple_of((par + m) % 2 * 512, 512), 512)
        cols = pl.ds(pl.multiple_of((x + d) % XS * PIECE, PIECE), PIECE)
        return jnp.dot(mixed[rows, :], wbuf[:, cols], preferred_element_type=jnp.float32)

    right = ((x + 1) % XS) * 2 + h
    left = ((x + XS - 1) % XS) * 2 + h
    upper, lower = pl.ds(0, TOK), pl.ds(TOK, TOK)

    def sends_over_x(m):
        far_out[m] = product(m, 2).astype(jnp.bfloat16)
        start(far_out.at[m, upper], far_up_in.at[m], x_send.at[m, 0], x_recv.at[m, 0], ctx, right)
        start(far_out.at[m, lower], far_down_in.at[m], x_send.at[m, 1], x_recv.at[m, 1], ctx, left)
        term = product(m, 1)
        up_out[m, lower] = term[TOK:].astype(jnp.bfloat16)
        arrived(far_up_in.at[m], x_recv.at[m, 0])
        up_out[m, upper] = (term[:TOK] + far_up_in[m].astype(jnp.float32)).astype(jnp.bfloat16)
        start(up_out.at[m], up_in.at[m], x_send.at[m, 2], x_recv.at[m, 2], ctx, right)
        term = product(m, 3)
        down_out[m, upper] = term[:TOK].astype(jnp.bfloat16)
        arrived(far_down_in.at[m], x_recv.at[m, 1])
        down_out[m, lower] = (term[TOK:] + far_down_in[m].astype(jnp.float32)).astype(jnp.bfloat16)
        start(down_out.at[m], down_in.at[m], x_send.at[m, 3], x_recv.at[m, 3], ctx, left)

    def sums_over_x(m):
        term = product(m, 0)
        arrived(up_in.at[m], x_recv.at[m, 2])
        arrived(down_in.at[m], x_recv.at[m, 3])
        both = up_in[m].astype(jnp.float32) + down_in[m].astype(jnp.float32)
        half_out[m] = (term + both).astype(jnp.bfloat16)
        for k in range(2):
            cc = (c + k) % 2
            rows = pl.ds(pl.multiple_of(cc * TOK, TOK), TOK)
            own_place = jnp.logical_and(m == 0 and k == 0, h == par)
            copy = remote(
                half_out.at[m, rows],
                half_in.at[h, c],
                h_send.at[m, k],
                h_recv.at[h, c],
                member((par + m) % 2, cc),
                x * 2 + par,
            )
            if m == 0 and k == 0:

                @pl.when(own_place)
                def _():
                    half_in[h, c] = half_out[m, rows]

                @pl.when(jnp.logical_not(own_place))
                def _():
                    copy.start()
            else:
                copy.start()
            last.append((copy, own_place if m == 0 and k == 0 else None))

    last = []
    sends_over_x(0)
    arrived(mixed.at[token_rows(1 - par, 1 - c)], mix_recv.at[2])
    sends_over_x(1)
    sums_over_x(0)
    sums_over_x(1)

    for a in range(2):
        for b in range(2):
            hs, cs = (h + a) % 2, (c + b) % 2
            if a == 0 and b == 0:

                @pl.when(par != h)
                def _():
                    arrived(half_in.at[hs, cs], h_recv.at[hs, cs])
            else:
                arrived(half_in.at[hs, cs], h_recv.at[hs, cs])
    for cs in range(2):
        out[:, cs * PIECE : (cs + 1) * PIECE] = (
            half_in[0, cs].astype(jnp.float32) + half_in[1, cs].astype(jnp.float32)
        ).astype(jnp.bfloat16)

    @pl.when(ctx < ZS * PLANE - 1)
    def _():
        halo_copy.wait_send()

    for copy in sent:
        copy.wait_send()
    for copy, own_place in last:
        if own_place is None:
            copy.wait_send()
        else:

            @pl.when(jnp.logical_not(own_place))
            def _():
                copy.wait_send()


def on_device(projected, short_filter, decay_rate, residue, skip_gain, out_weight):
    f32, bf16 = jnp.float32, jnp.bfloat16
    dma = pltpu.SemaphoreType.DMA
    scratch = [
        pltpu.VMEM((4, ROWS, 4 * PIECE), bf16),
        pltpu.VMEM((CHAN, 4 * PIECE), bf16),
        pltpu.VMEM((8, CHAN), f32),
        pltpu.VMEM((8, CHAN), f32),
        pltpu.VMEM((GROUPS * TOK, LANES), f32),
        pltpu.VMEM((TOK, CHAN), f32),
        pltpu.VMEM((GROUPS * TOK, LANES), f32),
        pltpu.VMEM((MODES * GROUPS, LANES), f32),
        pltpu.VMEM((MODES * GROUPS, LANES), f32),
        pltpu.VMEM((MODES * GROUPS, LANES), f32),
        pltpu.VMEM((MODES * GROUPS, LANES), f32),
        pltpu.VMEM((PLANE, 16, LANES), f32),
        pltpu.VMEM((16, LANES), f32),
        pltpu.VMEM((ZS, 16, LANES), f32),
        pltpu.VMEM((PLANE, 16, LANES), f32),
        pltpu.VMEM((MODES * GROUPS, LANES), f32),
        pltpu.VMEM((4 * TOK, CHAN), bf16),
        pltpu.VMEM((2, 2 * TOK, PIECE), bf16),
        pltpu.VMEM((2, 2 * TOK, PIECE), bf16),
        pltpu.VMEM((2, 2 * TOK, PIECE), bf16),
        pltpu.VMEM((2, TOK, PIECE), bf16),
        pltpu.VMEM((2, TOK, PIECE), bf16),
        pltpu.VMEM((2, 2 * TOK, PIECE), bf16),
        pltpu.VMEM((2, 2 * TOK, PIECE), bf16),
        pltpu.VMEM((2, 2 * TOK, PIECE), bf16),
        pltpu.VMEM((2, 2, TOK, PIECE), bf16),
        dma((2,)),
        dma((PLANE,)),
        dma((PLANE,)),
        dma((7,)),
        dma((7,)),
        dma((7,)),
        dma((7,)),
        dma((PLANE,)),
        dma((PLANE,)),
        dma((ZS,)),
        dma((ZS,)),
        dma((PLANE,)),
        dma((PLANE,)),
        dma((3,)),
        dma((3,)),
        dma((2, 4)),
        dma((2, 4)),
        dma((2, 2)),
        dma((2, 2)),
    ]
    return pl.pallas_call(
        block_kernel,
        out_shape=jax.ShapeDtypeStruct((TOK, 2 * PIECE), bf16),
        in_specs=[pl.BlockSpec(memory_space=pltpu.VMEM)] * 6,
        out_specs=pl.BlockSpec(memory_space=pltpu.VMEM),
        scratch_shapes=scratch,
        compiler_params=pltpu.CompilerParams(
            collective_id=0, has_side_effects=True, vmem_limit_bytes=40 * 1024 * 1024
        ),
    )(
        projected,
        short_filter,
        decay_rate.T,
        residue.T,
        skip_gain.reshape(GROUPS, LANES),
        out_weight,
    )


def solution(mesh):
    in_specs = (
        P(None, "ctx", "tp"),
        P(None, None, "tp"),
        P("tp", None),
        P("tp", None),
        P("tp"),
        P(("tp", "ctx"), None),
    )
    out_specs = P("ctx", "tp")
    return jax.shard_map(
        on_device, mesh=mesh, in_specs=in_specs, out_specs=out_specs, check_vma=False
    )
```

time: 287 us -> 97.1 us (0.34)
  the two profiles are of different devices: /device:TPU:1 before, /device:TPU:9 now
where the time goes in v1:
time: 97.1 us; the launch traced here: 96.8 us
  Pallas kernels  90.6 us (93%)
  local copies, waits for them, and re-layouts  6.18 us (6%)
    pallas_call x1, Pallas kernels, on_device(): pl.pallas_call(block_kernel, out_shape=jax.ShapeDtypeStruct((TOK, 2 * PIE...  90.6 us
    unnamed x13, local copies, waits for them, and re-layouts  6.18 us

profile of v1, /device:TPU:9, one launch (start us, length us, event | category | flops | bytes accessed | tf_op | source)
XLA Modules:
  0.0 96.8 jit_solution(88765159788294066)
XLA Ops:
  0.0 0.0 copy-start
  0.0 1.4 %copy-done = bf16[3,256,1024]{2,1,0:T(8,128)(2,1)S(1)} copy-done((bf16[3,256,1024]{2,1,0:T(8,128)(2,1)S(1)}, bf16[3,256,1024]{2,1,0:T(8,128)(2,1)}, u32[]{:S(2)}) %copy-start) | copy-done | bytes 1572888
  1.4 0.0 copy-start.1
  1.4 0.9 copy-done.1
  2.3 0.0 copy-start.2
  2.3 0.8 copy-done.2
  3.2 0.0 copy-start.3
  3.2 0.8 copy-done.3
  4.0 0.0 copy-start.4
  4.0 0.8 copy-done.4
  4.8 0.0 copy-start.5
  4.8 0.7 copy-done.5
  5.5 90.6 %shard_map.64 = bf16[256,512]{1,0:T(8,128)(2,1)S(1)} custom-call(bf16[3,256,1024]{2,1,0:T(8,128)(2,1)S(1)} %copy-done, f32[3,3,1024]{2,1,0:T(4,128)S(1)} %copy-done.4, f32[16,1024]{1,0:T(8,128)S(1)} %bitcast.3, f32[16,1024]{1,0:T(8,128)S(1)} %bitcast.4, f32[8,128]{1,0:T(8,128)S(1)} %bitcast.5, bf16[16,4096]{1,0:T(8,128)(2,1)S(1)} %copy-done.1), custom_call_target="tpu_custom_call" | custom-call | tf_op jit(solution)/shard_map/pallas_call | solution.py:519
  96.1 0.7 copy.8
Async XLA Ops:
  0.0 1.4 %copy-start = (bf16[3,256,1024]{2,1,0:T(8,128)(2,1)S(1)}, bf16[3,256,1024]{2,1,0:T(8,128)(2,1)}, u32[]{:S(2)}) copy-start(bf16[3,256,1024]{2,1,0:T(8,128)(2,1)} %proj.1) | copy-start | bytes 4718596
  1.4 0.9 copy-start.1
  2.3 0.8 copy-start.2
  3.2 0.8 copy-start.3
  4.0 0.8 copy-start.4
  4.8 0.7 copy-start.5

commit v2 on v1

v2 whole, which is shorter than its diff:
```python
import jax
import jax.numpy as jnp
from jax import lax
from jax.experimental import pallas as pl
from jax.experimental.pallas import tpu as pltpu
from jax.sharding import PartitionSpec as P

ZS = 8
PLANE = 8
XS = 4
TOK = 256
CHAN = 1024
LANES = 128
GROUPS = CHAN // LANES
MODES = 16
ROWS = 16
BLOCK = PLANE * ROWS
ORDER = (2, 1, 3, 0)
PIECE = 256
HEAD = 8
PARTS = ((0, 128), (128, 64), (192, 64))


def block_kernel(
    proj_hbm,
    filt_hbm,
    rate_hbm,
    resid_hbm,
    skip_hbm,
    weight_hbm,
    out,
    proj,
    filt,
    rate,
    resid,
    skip,
    weight,
    wq,
    wbuf,
    halo_out,
    halo_in,
    gates,
    query,
    conv,
    decay,
    gain,
    power,
    late,
    head,
    state,
    stage1,
    total,
    stage2,
    carries,
    carry,
    mixed,
    far_out,
    up_out,
    down_out,
    far_in,
    up_in,
    down_in,
    half_out,
    stay_sem,
    load_sem,
    halo_send,
    halo_recv,
    wy_send,
    wy_recv,
    up_send,
    up_recv,
    dn_send,
    dn_recv,
    s1_send,
    s1_recv,
    s2_send,
    s2_recv,
    s3_send,
    s3_recv,
    mix_send,
    mix_recv,
    x_send,
    x_recv,
    h_send,
    h_recv,
):
    ctx = lax.axis_index("ctx")
    tp = lax.axis_index("tp")
    z = ctx // PLANE
    e = ctx % PLANE
    c = e % 2
    par = (e // 2) % 2
    quad = e // 4
    x = tp // 2
    h = tp % 2

    def at(zz, ee):
        return zz * PLANE + ee

    def partner(k):
        return ((e // 4 + k // 4) % 2) * 4 + ((e // 2 + k // 2) % 2) * 2 + (e + k) % 2

    def member(pp, cc):
        return z * PLANE + quad * 4 + pp * 2 + cc

    def remote(src, dst, send, recv, to_ctx, to_tp):
        return pltpu.make_async_remote_copy(
            src_ref=src,
            dst_ref=dst,
            send_sem=send,
            recv_sem=recv,
            device_id={"ctx": to_ctx, "tp": to_tp},
            device_id_type=pl.DeviceIdType.MESH,
        )

    sent = []

    def start(*args):
        copy = remote(*args)
        copy.start()
        sent.append(copy)

    def arrived(dst, recv):
        remote(dst, dst, recv, recv, at((z + 1) % ZS, e), tp).wait_recv()

    barrier = pltpu.get_barrier_semaphore()

    def greet(to_ctx, to_tp):
        pl.semaphore_signal(
            barrier,
            inc=1,
            device_id={"ctx": to_ctx, "tp": to_tp},
            device_id_type=pl.DeviceIdType.MESH,
        )

    for k in range(1, PLANE):
        greet(at(z, (e + k) % PLANE), tp)
    for k in range(1, ZS):
        greet(at((z + k) % ZS, e), tp)
    for k in (1, XS - 1):
        greet(ctx, ((x + k) % XS) * 2 + h)
    for pp in range(2):
        for cc in range(2):
            greet(member(pp, cc), x * 2 + (1 - h))
    to_next = jnp.logical_and(e == PLANE - 1, z < ZS - 1)
    to_prev = jnp.logical_and(e == 0, z > 0)

    @pl.when(to_next)
    def _():
        greet(ctx + 1, tp)

    @pl.when(to_prev)
    def _():
        greet(ctx - 1, tp)

    loads = [
        pltpu.make_async_copy(src, dst, load_sem.at[k])
        for k, (src, dst) in enumerate(
            [
                (weight_hbm, weight),
                (proj_hbm.at[1], proj.at[1]),
                (proj_hbm.at[2], proj.at[2]),
                (proj_hbm.at[0], proj.at[0]),
                (rate_hbm, rate),
                (filt_hbm, filt),
                (resid_hbm, resid),
                (skip_hbm, skip),
            ]
        )
    ]
    for copy in loads:
        copy.start()

    loads[0].wait()
    for q in range(4):
        pp, cc = q // 2, q % 2
        for j in range(XS):
            col = (x + ORDER[j]) % XS * 1024 + pp * 512 + cc * PIECE
            wq[q, j] = weight[:, pl.ds(pl.multiple_of(col, PIECE), PIECE)]
    for k in range(1, 4):
        loads[k].wait()
    for p in range(3):
        rim = proj[p, TOK - 16 : TOK, :].astype(jnp.float32)
        halo_out[2 * p : 2 * p + 2, :] = rim[14:16, :]
    halo_out[6:8, :] = jnp.zeros((2, CHAN), jnp.float32)

    @pl.when(ctx == 0)
    def _():
        halo_in[...] = jnp.zeros_like(halo_in)

    beyond = jnp.logical_or(to_next, to_prev).astype(jnp.int32)
    pl.semaphore_wait(barrier, 7 + 7 + 2 + 4 + beyond)

    halo_copy = remote(halo_out, halo_in, halo_send.at[0], halo_recv.at[0], ctx + 1, tp)

    @pl.when(ctx < ZS * PLANE - 1)
    def _():
        halo_copy.start()

    my_rows = pl.ds(pl.multiple_of(z * BLOCK + e * ROWS, ROWS), ROWS)
    for group in range(2):
        js = pl.ds(2 * group, 2)
        for k in range(1, PLANE):
            ee = partner(k)
            share = ((ee // 2) % 2) * 2 + ee % 2
            start(
                wq.at[share, js],
                wbuf.at[js, my_rows],
                wy_send.at[group, k],
                wy_recv.at[group, k],
                at(z, ee),
                tp,
            )
    wbuf[:, my_rows, :] = wq[par * 2 + c]

    def piece(zz, j):
        return wbuf.at[j, pl.ds(pl.multiple_of(zz * BLOCK, BLOCK), BLOCK)]

    def up_hops(j):
        return 4 - j % 2

    def down_hops(j):
        return 3 + j % 2

    def pass_on(j, s):
        if s < up_hops(j):
            block = piece((z + ZS - s) % ZS, j)
            start(block, block, up_send.at[s, j], up_recv.at[s, j], at((z + 1) % ZS, e), tp)
        if s < down_hops(j):
            block = piece((z + s) % ZS, j)
            start(block, block, dn_send.at[s, j], dn_recv.at[s, j], at((z + ZS - 1) % ZS, e), tp)

    def begin(group):
        for k in range(1, PLANE):
            rows = pl.ds(pl.multiple_of(z * BLOCK + partner(k) * ROWS, ROWS), ROWS)
            arrived(wbuf.at[pl.ds(2 * group, 2), rows], wy_recv.at[group, k])
        pass_on(2 * group, 0)
        pass_on(2 * group + 1, 0)

    def forward(j, s):
        if s < up_hops(j):
            arrived(piece((z + 2 * ZS - 1 - s) % ZS, j), up_recv.at[s, j])
        if s < down_hops(j):
            arrived(piece((z + 1 + s) % ZS, j), dn_recv.at[s, j])
        pass_on(j, s + 1)

    for k in range(4, 8):
        loads[k].wait()
    for g in range(GROUPS):
        cols = slice(g * LANES, (g + 1) * LANES)
        places = pl.ds(g, MODES, stride=GROUPS)
        decay[places, :] = jnp.exp(-rate[:, cols])
        late[places, :] = jnp.exp(rate[:, cols] * (-float(TOK - HEAD)))
        power[places, :] = rate[:, cols]
        gain[places, :] = resid[:, cols]

    row_id = lax.broadcasted_iota(jnp.int32, (TOK, LANES), 0)

    def featured_part(p, cols):
        now = proj[p, :, cols].astype(jnp.float32)
        taps = filt[p, :, cols]
        one = jnp.where(row_id >= 1, pltpu.roll(now, 1, 0), 0.0)
        two = jnp.where(row_id >= 2, pltpu.roll(now, 2, 0), 0.0)
        return taps[0:1, :] * now + taps[1:2, :] * one + taps[2:3, :] * two

    def featurize_gates(g, carry_in):
        cols = pl.ds(pl.multiple_of(g * LANES, LANES), LANES)
        gates[pl.ds(pl.multiple_of(g * TOK, TOK), TOK), :] = (
            (featured_part(1, cols) * featured_part(2, cols)).astype(jnp.bfloat16)
        ).astype(jnp.float32)
        return carry_in

    def featurize_query(g, carry_in):
        cols = pl.ds(pl.multiple_of(g * LANES, LANES), LANES)
        query[:, cols] = featured_part(0, cols)
        return carry_in

    lax.fori_loop(0, GROUPS, featurize_gates, 0)

    def token(ref, t):
        return ref[pl.ds(t, GROUPS, stride=TOK), :]

    def mode(ref, n):
        return ref[n * GROUPS : (n + 1) * GROUPS, :]

    def summed(terms):
        while len(terms) > 1:
            terms = [
                terms[i] + terms[i + 1] if i + 1 < len(terms) else terms[i]
                for i in range(0, len(terms), 2)
            ]
        return terms[0]

    zero = tuple(jnp.zeros((GROUPS, LANES), jnp.float32) for _ in range(MODES))

    def local_filter(step, held):
        for u in range(HEAD):
            t = step * HEAD + u
            g_now = token(gates, t)
            held = tuple(mode(decay, n) * held[n] + g_now for n in range(MODES))
            terms = [mode(gain, n) * held[n] for n in range(MODES)]
            conv[pl.ds(t, GROUPS, stride=TOK), :] = summed(terms + [skip[...] * g_now])
        return held

    steps = TOK // HEAD
    tail = lax.fori_loop(1, steps // 2, local_filter, zero)
    tail = lax.fori_loop(steps // 2, steps, local_filter, tail)
    for n in range(MODES):
        state[n * GROUPS : (n + 1) * GROUPS, :] = tail[n]

    @pl.when(ctx > 0)
    def _():
        remote(halo_in, halo_in, halo_send.at[0], halo_recv.at[0], ctx - 1, tp).wait_recv()

    edge_id = lax.broadcasted_iota(jnp.int32, (HEAD, CHAN), 0)
    featured = []
    for p in range(3):
        now = proj[p, 0:16, :].astype(jnp.float32)[0:HEAD, :]
        before2 = halo_in[2 * p : 2 * p + 1, :]
        before1 = halo_in[2 * p + 1 : 2 * p + 2, :]
        one = jnp.where(edge_id >= 1, pltpu.roll(now, 1, 0), before1)
        two = jnp.where(
            edge_id >= 2, pltpu.roll(now, 2, 0), jnp.where(edge_id == 0, before2, before1)
        )
        taps = filt[p]
        featured.append(taps[0:1, :] * now + taps[1:2, :] * one + taps[2:3, :] * two)
    first = (featured[1] * featured[2]).astype(jnp.bfloat16).astype(jnp.float32)
    for g in range(GROUPS):
        gates[g * TOK : g * TOK + HEAD, :] = first[:, g * LANES : (g + 1) * LANES]
    opening = lax.fori_loop(0, 1, local_filter, zero)
    for n in range(MODES):
        rows = slice(n * GROUPS, (n + 1) * GROUPS)
        head[rows, :] = opening[n]
        state[rows, :] = state[rows, :] + late[rows, :] * opening[n]

    own_modes = pl.ds(pl.multiple_of(e * 16, 16), 16)
    for k in range(1, PLANE):
        ee = (e + k) % PLANE
        start(
            state.at[pl.ds(pl.multiple_of(ee * 16, 16), 16)],
            stage1.at[e],
            s1_send.at[k],
            s1_recv.at[k],
            at(z, ee),
            tp,
        )
    stage1[e] = state[own_modes, :]

    begin(0)
    begin(1)
    lax.fori_loop(0, GROUPS, featurize_query, 0)
    query[0:HEAD, :] = featured[0]
    forward(0, 0)
    forward(1, 0)

    for k in range(1, PLANE):
        arrived(stage1.at[(e + PLANE - k) % PLANE], s1_recv.at[k])
    rates = power[own_modes, :]
    over_device = jnp.exp(rates * (-float(TOK)))
    over_plane = jnp.exp(rates * (-float(TOK * PLANE)))
    running = stage1[0]
    for k in range(1, PLANE):
        running = over_device * running + stage1[k]
    total[...] = running
    for k in range(1, ZS):
        start(total, stage2.at[z], s2_send.at[k], s2_recv.at[k], at((z + k) % ZS, e), tp)
    stage2[z] = running

    forward(2, 0)
    forward(3, 0)
    forward(0, 1)
    forward(1, 1)

    for k in range(1, ZS):
        arrived(stage2.at[(z + ZS - k) % ZS], s2_recv.at[k])
    running = jnp.zeros((16, LANES), jnp.float32)
    for k in range(ZS - 1):
        running = jnp.where(k < z, over_plane * running + stage2[k], running)
    for k in range(PLANE):
        carries[k] = running
        if k < PLANE - 1:
            running = over_device * running + stage1[k]
    for k in range(1, PLANE):
        ee = (e + k) % PLANE
        start(carries.at[ee], carry.at[own_modes], s3_send.at[k], s3_recv.at[k], at(z, ee), tp)
    carry[own_modes, :] = carries[e]

    forward(2, 1)
    forward(3, 1)
    forward(0, 2)
    forward(1, 2)

    for k in range(1, PLANE):
        ee = (e + PLANE - k) % PLANE
        arrived(carry.at[pl.ds(pl.multiple_of(ee * 16, 16), 16)], s3_recv.at[k])

    def add_carry(step, held):
        for u in range(HEAD):
            t = step * HEAD + u
            held = tuple(mode(decay, n) * held[n] for n in range(MODES))
            conv[pl.ds(t, GROUPS, stride=TOK), :] = summed(list(held) + [token(conv, t)])
        return held

    across = member(1 - par, c)
    sibling = member(par, 1 - c)

    def direct(part):
        first, count = PARTS[part]
        return pl.ds(2 * TOK + 2 * first, count)

    def indirect(part):
        first, count = PARTS[part]
        return pl.ds(2 * TOK + 2 * first + count, count)

    def mix(part):
        first, count = PARTS[part]
        rows = slice(first, first + count)

        def mix_group(g, carry_in):
            cols = pl.ds(pl.multiple_of(g * LANES, LANES), LANES)
            places = pl.ds(pl.multiple_of(g * TOK + first, count), count)
            filtered = conv[places, :].astype(jnp.bfloat16).astype(jnp.float32)
            mixed[rows, cols] = (query[rows, cols] * filtered).astype(jnp.bfloat16)
            return carry_in

        lax.fori_loop(0, GROUPS, mix_group, 0)
        mine = mixed.at[pl.ds(first, count)]
        there = mixed.at[direct(part)]
        start(mine, there, mix_send.at[part, 0], mix_recv.at[part, 0], across, tp)
        there = mixed.at[pl.ds(TOK + first, count)]
        start(mine, there, mix_send.at[part, 1], mix_recv.at[part, 1], sibling, tp)

    held = tuple(mode(gain, n) * mode(carry, n) for n in range(MODES))
    held = lax.fori_loop(0, 1, add_carry, held)
    held = tuple(held[n] + mode(gain, n) * mode(head, n) for n in range(MODES))
    held = lax.fori_loop(1, steps // 2, add_carry, held)
    mix(0)
    forward(2, 2)
    forward(3, 2)
    held = lax.fori_loop(steps // 2, steps * 3 // 4, add_carry, held)
    mix(1)
    lax.fori_loop(steps * 3 // 4, steps, add_carry, held)
    mix(2)
    forward(0, 3)

    chunks = [(0, TOK), (TOK, TOK)] + [(2 * TOK + 2 * first, 2 * count) for first, count in PARTS]

    def product(m, d):
        first, count = chunks[m]
        return jnp.dot(
            mixed[first : first + count, :],
            wbuf[ORDER.index(d)],
            preferred_element_type=jnp.float32,
        )

    right = ((x + 1) % XS) * 2 + h
    left = ((x + XS - 1) % XS) * 2 + h

    def spans(m):
        first, count = chunks[m]
        half = count // 2
        return pl.ds(first, count), pl.ds(first, half), pl.ds(first + half, half), half

    def far_terms(m):
        every, upper, lower, _ = spans(m)
        far_out[every, :] = product(m, 2).astype(jnp.bfloat16)
        into = far_in.at[upper]
        start(far_out.at[upper], into, x_send.at[m, 0], x_recv.at[m, 0], ctx, right)
        into = far_in.at[lower]
        start(far_out.at[lower], into, x_send.at[m, 1], x_recv.at[m, 1], ctx, left)

    def near_terms(m):
        every, upper, lower, half = spans(m)
        term = product(m, 1)
        up_out[lower, :] = term[half:].astype(jnp.bfloat16)
        arrived(far_in.at[upper], x_recv.at[m, 0])
        up_out[upper, :] = (term[:half] + far_in[upper, :].astype(jnp.float32)).astype(jnp.bfloat16)
        start(up_out.at[every], up_in.at[every], x_send.at[m, 2], x_recv.at[m, 2], ctx, right)
        term = product(m, 3)
        down_out[upper, :] = term[:half].astype(jnp.bfloat16)
        arrived(far_in.at[lower], x_recv.at[m, 1])
        down_out[lower, :] = (term[half:] + far_in[lower, :].astype(jnp.float32)).astype(
            jnp.bfloat16
        )
        start(down_out.at[every], down_in.at[every], x_send.at[m, 3], x_recv.at[m, 3], ctx, left)

    last = []
    my_columns = pl.ds(pl.multiple_of(c * PIECE, PIECE), PIECE)
    stay = pltpu.make_async_copy(half_out.at[pl.ds(0, TOK)], out.at[h, :, my_columns], stay_sem)

    def own_terms(m):
        every, upper, lower, half = spans(m)
        term = product(m, 0)
        arrived(up_in.at[every], x_recv.at[m, 2])
        arrived(down_in.at[every], x_recv.at[m, 3])
        both = up_in[every, :].astype(jnp.float32) + down_in[every, :].astype(jnp.float32)
        half_out[every, :] = (term + both).astype(jnp.bfloat16)
        if m < 2:
            moves = [(member(par, (c + m) % 2), every, pl.ds(0, TOK), 3)]
        else:
            place = pl.ds(*PARTS[m - 2])
            moves = [
                (member(1 - par, c), upper, place, m - 2),
                (member(1 - par, 1 - c), lower, place, m - 2),
            ]
        for k, (to, rows, place, slot) in enumerate(moves):
            copy = remote(
                half_out.at[rows],
                out.at[h, place, my_columns],
                h_send.at[m, k],
                h_recv.at[h, c, slot],
                to,
                x * 2 + par,
            )
            if m == 0:

                @pl.when(h == par)
                def _():
                    stay.start()

                @pl.when(h != par)
                def _():
                    copy.start()
            else:
                copy.start()
            last.append((copy, m == 0))

    def from_across(part):
        rows = direct(part)
        arrived(mixed.at[rows], mix_recv.at[part, 0])
        there = mixed.at[indirect(part)]
        start(mixed.at[rows], there, mix_send.at[part, 2], mix_recv.at[part, 2], sibling, tp)

    def from_sibling(part):
        arrived(mixed.at[indirect(part)], mix_recv.at[part, 2])

    far_terms(0)
    for part, (first, count) in enumerate(PARTS):
        arrived(mixed.at[pl.ds(TOK + first, count)], mix_recv.at[part, 1])
    far_terms(1)
    forward(1, 3)
    forward(2, 3)
    near_terms(0)
    from_across(0)
    near_terms(1)
    from_sibling(0)
    far_terms(2)
    from_across(1)
    forward(3, 3)
    own_terms(0)
    from_sibling(1)
    far_terms(3)
    from_across(2)
    near_terms(2)
    from_sibling(2)
    far_terms(4)
    own_terms(1)
    near_terms(3)
    near_terms(4)
    own_terms(2)
    own_terms(3)
    own_terms(4)

    for k in range(4):
        hs, cs = (h + k // 2) % 2, (c + k) % 2
        columns = pl.ds(pl.multiple_of(cs * PIECE, PIECE), PIECE)
        if k > 0:

            @pl.when(par == h)
            def _(hs=hs, cs=cs, columns=columns):
                arrived(out.at[hs, :, columns], h_recv.at[hs, cs, 3])

        @pl.when(par != h)
        def _(hs=hs, cs=cs, columns=columns):
            for part, (first, count) in enumerate(PARTS):
                arrived(out.at[hs, pl.ds(first, count), columns], h_recv.at[hs, cs, part])

    @pl.when(h == par)
    def _():
        stay.wait()

    @pl.when(ctx < ZS * PLANE - 1)
    def _():
        halo_copy.wait_send()

    for copy in sent:
        copy.wait_send()
    for copy, may_stay in last:
        if may_stay:

            @pl.when(h != par)
            def _():
                copy.wait_send()
        else:
            copy.wait_send()


def on_device(projected, short_filter, decay_rate, residue, skip_gain, out_weight):
    f32, bf16 = jnp.float32, jnp.bfloat16
    dma = pltpu.SemaphoreType.DMA
    table = pltpu.VMEM((MODES * GROUPS, LANES), f32)
    sums = pltpu.VMEM((4 * TOK, PIECE), bf16)
    scratch = [
        pltpu.VMEM((3, TOK, CHAN), bf16),
        pltpu.VMEM((3, 3, CHAN), f32),
        pltpu.VMEM((MODES, CHAN), f32),
        pltpu.VMEM((MODES, CHAN), f32),
        pltpu.VMEM((GROUPS, LANES), f32),
        pltpu.VMEM((ROWS, 4096), bf16),
        pltpu.VMEM((4, XS, ROWS, PIECE), bf16),
        pltpu.VMEM((XS, CHAN, PIECE), bf16),
        pltpu.VMEM((8, CHAN), f32),
        pltpu.VMEM((8, CHAN), f32),
        pltpu.VMEM((GROUPS * TOK, LANES), f32),
        pltpu.VMEM((TOK, CHAN), f32),
        pltpu.VMEM((GROUPS * TOK, LANES), f32),
        table,
        table,
        table,
        table,
        table,
        table,
        pltpu.VMEM((PLANE, 16, LANES), f32),
        pltpu.VMEM((16, LANES), f32),
        pltpu.VMEM((ZS, 16, LANES), f32),
        pltpu.VMEM((PLANE, 16, LANES), f32),
        table,
        pltpu.VMEM((4 * TOK, CHAN), bf16),
        sums,
        sums,
        sums,
        sums,
        sums,
        sums,
        sums,
        dma,
        dma((8,)),
        dma((1,)),
        dma((1,)),
        dma((2, PLANE)),
        dma((2, PLANE)),
        dma((4, 4)),
        dma((4, 4)),
        dma((4, 4)),
        dma((4, 4)),
        dma((PLANE,)),
        dma((PLANE,)),
        dma((ZS,)),
        dma((ZS,)),
        dma((PLANE,)),
        dma((PLANE,)),
        dma((3, 3)),
        dma((3, 3)),
        dma((5, 4)),
        dma((5, 4)),
        dma((5, 2)),
        dma((2, 2, 4)),
    ]
    halves = pl.pallas_call(
        block_kernel,
        out_shape=jax.ShapeDtypeStruct((2, TOK, 2 * PIECE), bf16),
        in_specs=[pl.BlockSpec(memory_space=pltpu.HBM)] * 6,
        out_specs=pl.BlockSpec(memory_space=pltpu.HBM),
        scratch_shapes=scratch,
        compiler_params=pltpu.CompilerParams(
            collective_id=0, has_side_effects=True, vmem_limit_bytes=61 * 1024 * 1024
        ),
    )(
        projected,
        short_filter,
        decay_rate.T,
        residue.T,
        skip_gain.reshape(GROUPS, LANES),
        out_weight,
    )
    return (halves[0].astype(f32) + halves[1].astype(f32)).astype(bf16)


def solution(mesh):
    in_specs = (
        P(None, "ctx", "tp"),
        P(None, None, "tp"),
        P("tp", None),
        P("tp", None),
        P("tp"),
        P(("tp", "ctx"), None),
    )
    out_specs = P("ctx", "tp")
    return jax.shard_map(
        on_device, mesh=mesh, in_specs=in_specs, out_specs=out_specs, check_vma=False
    )
```

time: 97.1 us -> 77.6 us (0.80)
  the two profiles are of different devices: /device:TPU:9 before, /device:TPU:49 now
where the time goes in v2:
time: 77.6 us; the launch traced here: 77.5 us
  Pallas kernels  75.7 us (98%)
  other arithmetic  1.8 us (2%)
    pallas_call x1, Pallas kernels, on_device(): pl.pallas_call(block_kernel, out_shape=jax.ShapeDtypeStruct((2, TOK, 2 *...  75.7 us
    convert_element_type x1, other arithmetic, on_device(): return (halves[0].astype(f32) + halves[1].astype(f32)).astype(bf16)  1.8 us

profile of v2, /device:TPU:49, one launch (start us, length us, event | category | flops | bytes accessed | tf_op | source)
XLA Modules:
  0.0 77.5 jit_solution(6906657774017799177)
XLA Ops:
  0.0 75.7 %shard_map.64 = bf16[2,256,512]{2,1,0:T(8,128)(2,1)} custom-call(bf16[3,256,1024]{2,1,0:T(8,128)(2,1)} %proj_hbm.1, f32[3,3,1024]{2,1,0:T(4,128)} %filt_hbm.1, f32[16,1024]{1,0:T(8,128)} %bitcast.5, f32[16,1024]{1,0:T(8,128)} %bitcast.6, f32[8,128]{1,0:T(8,128)} %bitcast.7, bf16[16,4096]{1,0:T(8,128)(2,1)} %weight_hbm.1), custom_call_target="tpu_custom_call" | custom-call | tf_op jit(solution)/shard_map/pallas_call | solution.py:659
  75.7 1.8 %fusion = bf16[256,512]{1,0:T(8,128)(2,1)} fusion(bf16[2,256,512]{2,1,0:T(8,128)(2,1)} %shard_map.64), kind=kLoop, calls=%fused_computation.1 | loop fusion | flops 524288 | bytes 786432 | tf_op jit(solution)/shard_map/convert_element_type | solution.py:676

commit v3 on v2

--- a/solution.py
+++ b/solution.py
@@ -175,8 +175,11 @@
     for q in range(4):
         pp, cc = q // 2, q % 2
         for j in range(XS):
-            col = (x + ORDER[j]) % XS * 1024 + pp * 512 + cc * PIECE
-            wq[q, j] = weight[:, pl.ds(pl.multiple_of(col, PIECE), PIECE)]
+            for hh in range(2):
+                col = (x + ORDER[j]) % XS * 1024 + hh * 512 + (pp * 2 + cc) * LANES
+                wq[q, j, :, hh * LANES : (hh + 1) * LANES] = weight[
+                    :, pl.ds(pl.multiple_of(col, LANES), LANES)
+                ]
     for k in range(1, 4):
         loads[k].wait()
     for p in range(3):
@@ -198,8 +201,10 @@
         halo_copy.start()
 
     my_rows = pl.ds(pl.multiple_of(z * BLOCK + e * ROWS, ROWS), ROWS)
-    for group in range(2):
-        js = pl.ds(2 * group, 2)
+    groups = (pl.ds(0, 3), pl.ds(3, 1))
+
+    def plane_shares(group):
+        js = groups[group]
         for k in range(1, PLANE):
             ee = partner(k)
             share = ((ee // 2) % 2) * 2 + ee % 2
@@ -211,6 +216,8 @@
                 at(z, ee),
                 tp,
             )
+
+    plane_shares(0)
     wbuf[:, my_rows, :] = wq[par * 2 + c]
 
     def piece(zz, j):
@@ -233,9 +240,9 @@
     def begin(group):
         for k in range(1, PLANE):
             rows = pl.ds(pl.multiple_of(z * BLOCK + partner(k) * ROWS, ROWS), ROWS)
-            arrived(wbuf.at[pl.ds(2 * group, 2), rows], wy_recv.at[group, k])
-        pass_on(2 * group, 0)
-        pass_on(2 * group + 1, 0)
+            arrived(wbuf.at[groups[group], rows], wy_recv.at[group, k])
+        for j in (range(3), range(3, 4))[group]:
+            pass_on(j, 0)
 
     def forward(j, s):
         if s < up_hops(j):
@@ -346,12 +353,11 @@
         )
     stage1[e] = state[own_modes, :]
 
-    begin(0)
-    begin(1)
     lax.fori_loop(0, GROUPS, featurize_query, 0)
     query[0:HEAD, :] = featured[0]
+    begin(0)
+    plane_shares(1)
     forward(0, 0)
-    forward(1, 0)
 
     for k in range(1, PLANE):
         arrived(stage1.at[(e + PLANE - k) % PLANE], s1_recv.at[k])
@@ -366,10 +372,9 @@
         start(total, stage2.at[z], s2_send.at[k], s2_recv.at[k], at((z + k) % ZS, e), tp)
     stage2[z] = running
 
+    forward(1, 0)
     forward(2, 0)
-    forward(3, 0)
     forward(0, 1)
-    forward(1, 1)
 
     for k in range(1, ZS):
         arrived(stage2.at[(z + ZS - k) % ZS], s2_recv.at[k])
@@ -385,10 +390,10 @@
         start(carries.at[ee], carry.at[own_modes], s3_send.at[k], s3_recv.at[k], at(z, ee), tp)
     carry[own_modes, :] = carries[e]
 
+    forward(1, 1)
     forward(2, 1)
-    forward(3, 1)
     forward(0, 2)
-    forward(1, 2)
+    begin(1)
 
     for k in range(1, PLANE):
         ee = (e + PLANE - k) % PLANE
@@ -435,8 +440,8 @@
     held = tuple(held[n] + mode(gain, n) * mode(head, n) for n in range(MODES))
     held = lax.fori_loop(1, steps // 2, add_carry, held)
     mix(0)
+    forward(1, 2)
     forward(2, 2)
-    forward(3, 2)
     held = lax.fori_loop(steps // 2, steps * 3 // 4, add_carry, held)
     mix(1)
     lax.fori_loop(steps * 3 // 4, steps, add_carry, held)
@@ -485,8 +490,14 @@
         start(down_out.at[every], down_in.at[every], x_send.at[m, 3], x_recv.at[m, 3], ctx, left)
 
     last = []
-    my_columns = pl.ds(pl.multiple_of(c * PIECE, PIECE), PIECE)
-    stay = pltpu.make_async_copy(half_out.at[pl.ds(0, TOK)], out.at[h, :, my_columns], stay_sem)
+    my_columns = pl.ds(pl.multiple_of((par * 2 + c) * LANES, LANES), LANES)
+
+    def of_half(hh):
+        return pl.ds(pl.multiple_of(hh * LANES, LANES), LANES)
+
+    stay = pltpu.make_async_copy(
+        half_out.at[pl.ds(0, TOK), of_half(h)], out.at[h, :, my_columns], stay_sem
+    )
 
     def own_terms(m):
         every, upper, lower, half = spans(m)
@@ -503,27 +514,22 @@
                 (member(1 - par, c), upper, place, m - 2),
                 (member(1 - par, 1 - c), lower, place, m - 2),
             ]
-        for k, (to, rows, place, slot) in enumerate(moves):
-            copy = remote(
-                half_out.at[rows],
-                out.at[h, place, my_columns],
-                h_send.at[m, k],
-                h_recv.at[h, c, slot],
-                to,
-                x * 2 + par,
-            )
-            if m == 0:
-
-                @pl.when(h == par)
-                def _():
+        for a in (1, 0):
+            hh = (h + a) % 2
+            for k, (to, rows, place, slot) in enumerate(moves):
+                if m == 0 and a == 0:
                     stay.start()
-
-                @pl.when(h != par)
-                def _():
-                    copy.start()
-            else:
+                    continue
+                copy = remote(
+                    half_out.at[rows, of_half(hh)],
+                    out.at[h, place, my_columns],
+                    h_send.at[m, a, k],
+                    h_recv.at[h, par * 2 + c, slot],
+                    to,
+                    x * 2 + hh,
+                )
                 copy.start()
-            last.append((copy, m == 0))
+                last.append(copy)
 
     def from_across(part):
         rows = direct(part)
@@ -538,11 +544,14 @@
     for part, (first, count) in enumerate(PARTS):
         arrived(mixed.at[pl.ds(TOK + first, count)], mix_recv.at[part, 1])
     far_terms(1)
+    forward(3, 0)
     forward(1, 3)
     forward(2, 3)
     near_terms(0)
+    forward(3, 1)
     from_across(0)
     near_terms(1)
+    forward(3, 2)
     from_sibling(0)
     far_terms(2)
     from_across(1)
@@ -561,23 +570,17 @@
     own_terms(3)
     own_terms(4)
 
-    for k in range(4):
-        hs, cs = (h + k // 2) % 2, (c + k) % 2
-        columns = pl.ds(pl.multiple_of(cs * PIECE, PIECE), PIECE)
-        if k > 0:
-
-            @pl.when(par == h)
-            def _(hs=hs, cs=cs, columns=columns):
-                arrived(out.at[hs, :, columns], h_recv.at[hs, cs, 3])
-
-        @pl.when(par != h)
-        def _(hs=hs, cs=cs, columns=columns):
+    for k in range(8):
+        hs, ps, cs = (h + k // 4) % 2, (par + k // 2) % 2, (c + k) % 2
+        columns = pl.ds(pl.multiple_of((ps * 2 + cs) * LANES, LANES), LANES)
+        if k == 0:
+            stay.wait()
+        elif k // 2 % 2 == 0:
+            arrived(out.at[hs, :, columns], h_recv.at[hs, ps * 2 + cs, 3])
+        else:
             for part, (first, count) in enumerate(PARTS):
-                arrived(out.at[hs, pl.ds(first, count), columns], h_recv.at[hs, cs, part])
-
-    @pl.when(h == par)
-    def _():
-        stay.wait()
+                place = out.at[hs, pl.ds(first, count), columns]
+                arrived(place, h_recv.at[hs, ps * 2 + cs, part])
 
     @pl.when(ctx < ZS * PLANE - 1)
     def _():
@@ -585,14 +588,8 @@
 
     for copy in sent:
         copy.wait_send()
-    for copy, may_stay in last:
-        if may_stay:
-
-            @pl.when(h != par)
-            def _():
-                copy.wait_send()
-        else:
-            copy.wait_send()
+    for copy in last:
+        copy.wait_send()
 
 
 def on_device(projected, short_filter, decay_rate, residue, skip_gain, out_weight):
@@ -653,8 +650,8 @@
         dma((3, 3)),
         dma((5, 4)),
         dma((5, 4)),
-        dma((5, 2)),
-        dma((2, 2, 4)),
+        dma((5, 2, 2)),
+        dma((2, 4, 4)),
     ]
     halves = pl.pallas_call(
         block_kernel,

time: 77.6 us -> 71.2 us (0.918)
  the two profiles are of different devices: /device:TPU:49 before, /device:TPU:1 now
where the time goes in v3:
time: 71.2 us; the launch traced here: 71.1 us
  Pallas kernels  69.3 us (97%)
  other arithmetic  1.8 us (3%)
    pallas_call x1, Pallas kernels, on_device(): pl.pallas_call(block_kernel, out_shape=jax.ShapeDtypeStruct((2, TOK, 2 *...  69.3 us
    convert_element_type x1, other arithmetic, on_device(): return (halves[0].astype(f32) + halves[1].astype(f32)).astype(bf16)  1.8 us

profile of v3, /device:TPU:1, one launch (start us, length us, event | category | flops | bytes accessed | tf_op | source)
XLA Modules:
  0.0 71.1 jit_solution(10458860948370684366)
XLA Ops:
  0.0 69.3 %shard_map.64 = bf16[2,256,512]{2,1,0:T(8,128)(2,1)} custom-call(bf16[3,256,1024]{2,1,0:T(8,128)(2,1)} %proj_hbm.1, f32[3,3,1024]{2,1,0:T(4,128)} %filt_hbm.1, f32[16,1024]{1,0:T(8,128)} %bitcast.5, f32[16,1024]{1,0:T(8,128)} %bitcast.6, f32[8,128]{1,0:T(8,128)} %bitcast.7, bf16[16,4096]{1,0:T(8,128)(2,1)} %weight_hbm.1), custom_call_target="tpu_custom_call" | custom-call | tf_op jit(solution)/shard_map/pallas_call | solution.py:656
  69.3 1.8 %fusion = bf16[256,512]{1,0:T(8,128)(2,1)} fusion(bf16[2,256,512]{2,1,0:T(8,128)(2,1)} %shard_map.64), kind=kLoop, calls=%fused_computation.1 | loop fusion | flops 524288 | bytes 786432 | tf_op jit(solution)/shard_map/convert_element_type | solution.py:673

commit v4 on v3

--- a/solution.py
+++ b/solution.py
@@ -440,12 +440,12 @@
     held = tuple(held[n] + mode(gain, n) * mode(head, n) for n in range(MODES))
     held = lax.fori_loop(1, steps // 2, add_carry, held)
     mix(0)
-    forward(1, 2)
-    forward(2, 2)
     held = lax.fori_loop(steps // 2, steps * 3 // 4, add_carry, held)
     mix(1)
     lax.fori_loop(steps * 3 // 4, steps, add_carry, held)
     mix(2)
+    forward(1, 2)
+    forward(2, 2)
     forward(0, 3)
 
     chunks = [(0, TOK), (TOK, TOK)] + [(2 * TOK + 2 * first, 2 * count) for first, count in PARTS]
@@ -595,7 +595,8 @@
 def on_device(projected, short_filter, decay_rate, residue, skip_gain, out_weight):
     f32, bf16 = jnp.float32, jnp.bfloat16
     dma = pltpu.SemaphoreType.DMA
-    table = pltpu.VMEM((MODES * GROUPS, LANES), f32)
+    table = pltpu.VMEM(((MODES + 1) * GROUPS, LANES), f32)
+    by_token = pltpu.VMEM(((GROUPS + 1) * TOK, LANES), f32)
     sums = pltpu.VMEM((4 * TOK, PIECE), bf16)
     scratch = [
         pltpu.VMEM((3, TOK, CHAN), bf16),
@@ -608,9 +609,9 @@
         pltpu.VMEM((XS, CHAN, PIECE), bf16),
         pltpu.VMEM((8, CHAN), f32),
         pltpu.VMEM((8, CHAN), f32),
-        pltpu.VMEM((GROUPS * TOK, LANES), f32),
+        by_token,
         pltpu.VMEM((TOK, CHAN), f32),
-        pltpu.VMEM((GROUPS * TOK, LANES), f32),
+        by_token,
         table,
         table,
         table,

time: 71.2 us -> 71 us (level)
  no operation moved by 1% of the time
where the time goes in v4:
time: 71 us; the launch traced here: 70.8 us
  Pallas kernels  69 us (97%)
  other arithmetic  1.8 us (3%)
    pallas_call x1, Pallas kernels, on_device(): pl.pallas_call(block_kernel, out_shape=jax.ShapeDtypeStruct((2, TOK, 2 *...  69 us
    convert_element_type x1, other arithmetic, on_device(): return (halves[0].astype(f32) + halves[1].astype(f32)).astype(bf16)  1.8 us

profile of v4, /device:TPU:1, one launch (start us, length us, event | category | flops | bytes accessed | tf_op | source)
XLA Modules:
  0.0 70.8 jit_solution(14797474966338483032)
XLA Ops:
  0.0 69.0 %shard_map.64 = bf16[2,256,512]{2,1,0:T(8,128)(2,1)} custom-call(bf16[3,256,1024]{2,1,0:T(8,128)(2,1)} %proj_hbm.1, f32[3,3,1024]{2,1,0:T(4,128)} %filt_hbm.1, f32[16,1024]{1,0:T(8,128)} %bitcast.5, f32[16,1024]{1,0:T(8,128)} %bitcast.6, f32[8,128]{1,0:T(8,128)} %bitcast.7, bf16[16,4096]{1,0:T(8,128)(2,1)} %weight_hbm.1), custom_call_target="tpu_custom_call" | custom-call | tf_op jit(solution)/shard_map/pallas_call | solution.py:657
  69.0 1.8 %fusion = bf16[256,512]{1,0:T(8,128)(2,1)} fusion(bf16[2,256,512]{2,1,0:T(8,128)(2,1)} %shard_map.64), kind=kLoop, calls=%fused_computation.1 | loop fusion | flops 524288 | bytes 786432 | tf_op jit(solution)/shard_map/convert_element_type | solution.py:674

commit v5 on v4

--- a/solution.py
+++ b/solution.py
@@ -30,6 +30,7 @@
     weight_hbm,
     out,
     proj,
+    rims,
     filt,
     rate,
     resid,
@@ -158,6 +159,7 @@
         for k, (src, dst) in enumerate(
             [
                 (weight_hbm, weight),
+                (proj_hbm.at[:, pl.ds(TOK - 16, 16)], rims),
                 (proj_hbm.at[1], proj.at[1]),
                 (proj_hbm.at[2], proj.at[2]),
                 (proj_hbm.at[0], proj.at[0]),
@@ -180,10 +182,9 @@
                 wq[q, j, :, hh * LANES : (hh + 1) * LANES] = weight[
                     :, pl.ds(pl.multiple_of(col, LANES), LANES)
                 ]
-    for k in range(1, 4):
-        loads[k].wait()
+    loads[1].wait()
     for p in range(3):
-        rim = proj[p, TOK - 16 : TOK, :].astype(jnp.float32)
+        rim = rims[p].astype(jnp.float32)
         halo_out[2 * p : 2 * p + 2, :] = rim[14:16, :]
     halo_out[6:8, :] = jnp.zeros((2, CHAN), jnp.float32)
 
@@ -251,7 +252,7 @@
             arrived(piece((z + 1 + s) % ZS, j), dn_recv.at[s, j])
         pass_on(j, s + 1)
 
-    for k in range(4, 8):
+    for k in range(2, 9):
         loads[k].wait()
     for g in range(GROUPS):
         cols = slice(g * LANES, (g + 1) * LANES)
@@ -368,8 +369,11 @@
     for k in range(1, PLANE):
         running = over_device * running + stage1[k]
     total[...] = running
+    onward = []
     for k in range(1, ZS):
-        start(total, stage2.at[z], s2_send.at[k], s2_recv.at[k], at((z + k) % ZS, e), tp)
+        copy = remote(total, stage2.at[z], s2_send.at[k], s2_recv.at[k], at((z + k) % ZS, e), tp)
+        pl.when(z + k < ZS)(copy.start)
+        onward.append((k, copy))
     stage2[z] = running
 
     forward(1, 0)
@@ -377,7 +381,11 @@
     forward(0, 1)
 
     for k in range(1, ZS):
-        arrived(stage2.at[(z + ZS - k) % ZS], s2_recv.at[k])
+
+        @pl.when(z >= k)
+        def _(k=k):
+            arrived(stage2.at[(z + ZS - k) % ZS], s2_recv.at[k])
+
     running = jnp.zeros((16, LANES), jnp.float32)
     for k in range(ZS - 1):
         running = jnp.where(k < z, over_plane * running + stage2[k], running)
@@ -590,6 +598,8 @@
         copy.wait_send()
     for copy in last:
         copy.wait_send()
+    for k, copy in onward:
+        pl.when(z + k < ZS)(copy.wait_send)
 
 
 def on_device(projected, short_filter, decay_rate, residue, skip_gain, out_weight):
@@ -600,6 +610,7 @@
     sums = pltpu.VMEM((4 * TOK, PIECE), bf16)
     scratch = [
         pltpu.VMEM((3, TOK, CHAN), bf16),
+        pltpu.VMEM((3, 16, CHAN), bf16),
         pltpu.VMEM((3, 3, CHAN), f32),
         pltpu.VMEM((MODES, CHAN), f32),
         pltpu.VMEM((MODES, CHAN), f32),
@@ -632,7 +643,7 @@
         sums,
         sums,
         dma,
-        dma((8,)),
+        dma((9,)),
         dma((1,)),
         dma((1,)),
         dma((2, PLANE)),

time: 71 us -> 71.7 us (level)
  Pallas kernels: 69 us -> 69.8 us
    pallas_call x1, Pallas kernels: 69 us -> 69.8 us  [on_device(): pl.pallas_call(block_kernel, out_shape=jax.ShapeDtypeStruct((2, TOK, 2 *...]
where the time goes in v5:
time: 71.7 us; the launch traced here: 71.6 us
  Pallas kernels  69.8 us (97%)
  other arithmetic  1.8 us (3%)
    pallas_call x1, Pallas kernels, on_device(): pl.pallas_call(block_kernel, out_shape=jax.ShapeDtypeStruct((2, TOK, 2 *...  69.8 us
    convert_element_type x1, other arithmetic, on_device(): return (halves[0].astype(f32) + halves[1].astype(f32)).astype(bf16)  1.8 us

profile of v5, /device:TPU:1, one launch (start us, length us, event | category | flops | bytes accessed | tf_op | source)
XLA Modules:
  0.0 71.6 jit_solution(14057175893139101246)
XLA Ops:
  0.0 69.8 %shard_map.64 = bf16[2,256,512]{2,1,0:T(8,128)(2,1)} custom-call(bf16[3,256,1024]{2,1,0:T(8,128)(2,1)} %proj_hbm.1, f32[3,3,1024]{2,1,0:T(4,128)} %filt_hbm.1, f32[16,1024]{1,0:T(8,128)} %bitcast.5, f32[16,1024]{1,0:T(8,128)} %bitcast.6, f32[8,128]{1,0:T(8,128)} %bitcast.7, bf16[16,4096]{1,0:T(8,128)(2,1)} %weight_hbm.1), custom_call_target="tpu_custom_call" | custom-call | tf_op jit(solution)/shard_map/pallas_call | solution.py:668
  69.8 1.8 %fusion = bf16[256,512]{1,0:T(8,128)(2,1)} fusion(bf16[2,256,512]{2,1,0:T(8,128)(2,1)} %shard_map.64), kind=kLoop, calls=%fused_computation.1 | loop fusion | flops 524288 | bytes 786432 | tf_op jit(solution)/shard_map/convert_element_type | solution.py:685
